TPU v7x, 512 devices: a whole 4x4x16 slice. The times are simulated.
512 devices in a mesh: band: 64 (over x, z), ens: 8 (over y, core).
Axes of the slice: x: 4, y: 4, z: 16, core: 2. Of those that a mesh axis runs over, the one named last changes fastest.
Arguments:
- state: bfloat16 [8, 114, 368640], P('ens', None, 'band'), may hold values from -6 to 6
- cotangent: bfloat16 [8, 114, 368640], P('ens', None, 'band'), may hold values from -6 to 6
- w_in: bfloat16 [114, 384], replicated, may hold values from -0.5 to 0.5
- b_in: float32 [384], replicated, may hold values from -3 to 3
- w_out: bfloat16 [114, 384], replicated, may hold values from -0.3125 to 0.3125
- legendre: bfloat16 [256, 256, 256], P('band'), may hold values from -2 to 2
- diffusion: float32 [114], replicated, may hold values from 0.3 to 30
- quad: float32 [256], replicated, may hold values from 0.3 to 3
- table: int32 [64, 4], replicated, may hold values from 0 to 255, as said below
Outputs:
- state_grad: bfloat16 [8, 114, 368640], P('ens', None, 'band')
- w_in_grad: float32 [114, 384], replicated
- w_out_grad: float32 [114, 384], replicated
- b_in_grad: float32 [384], replicated
Inputs may be any that keep to these rules, and one draw needn't show every extreme that they name: `table`: each wavenumber 0 to 255 appears exactly once. Columns 2g and 2g+1 of every row hold m and (4 g + 2) * 64 - 1 - m for some m with 2 g * 64 <= m < (2 g + 1) * 64, so the sum of 256 - m over the wavenumbers m of a row is the same for every row.
All inputs are finite; a program needn't handle non-finite values.
Results may differ from a plain program's by a relative error of at most 0.018.
Values may be sent and summed in bfloat16 or wider, within the bound.
A program may use at most 64 MiB of HBM per device.

v0:
```python
import math

import jax
import jax.numpy as jnp
from jax import lax
from jax.sharding import PartitionSpec as P

NLON = 1440


def wave_matrix(table):
    wavenumbers = table.reshape(-1)
    longitude = jnp.arange(NLON, dtype=jnp.int32)
    phase = wavenumbers[:, None] * longitude[None, :] % NLON
    angle = phase.astype(jnp.float32) * (2.0 * math.pi / NLON)
    stacked = jnp.stack([jnp.cos(angle), jnp.sin(angle)], axis=1)
    stacked = stacked.reshape(2 * wavenumbers.shape[0], NLON)
    return (stacked * (1.0 / math.sqrt(NLON))).astype(jnp.bfloat16)


def damping_table(wavenumbers, diffusion, degrees):
    degree = jnp.arange(degrees, dtype=jnp.float32)
    scaled = degree * (degree + 1.0) / (degrees * (degrees - 1.0))
    keeping = (jnp.arange(degrees, dtype=jnp.int32)[None, :] >= wavenumbers[:, None]).astype(
        jnp.float32
    )
    return keeping[:, None, :] / (1.0 + diffusion[None, :, None] * (scaled * scaled)[None, None, :])


def add_coefs(first, second):
    return (first.astype(jnp.float32) + second.astype(jnp.float32)).astype(jnp.bfloat16)


def body(state, cotangent, w_in, b_in, w_out, legendre, diffusion, quad, table):
    channels = state.shape[1]
    band_count = lax.axis_size("band")
    position = lax.axis_index("band")
    slots = legendre.shape[0]
    nlat = legendre.shape[1]
    degrees = legendre.shape[2]
    lat_dev = nlat // band_count
    wave_rows = wave_matrix(table)
    own_modes = lax.dynamic_slice_in_dim(table, position, 1, 0)[0]
    damping = damping_table(own_modes, diffusion, degrees)
    quad_rows = lax.dynamic_slice_in_dim(quad, position * lat_dev, lat_dev, 0)
    state_field = state[0].reshape(channels, lat_dev, NLON)
    cot_field = cotangent[0].reshape(channels, lat_dev, NLON)

    def analysis(field):
        return jnp.einsum("cln,kn->kcl", field, wave_rows, preferred_element_type=jnp.float32)

    def synthesis(coefs):
        return jnp.einsum("kcl,kn->cln", coefs, wave_rows, preferred_element_type=jnp.float32)

    def legendre_pass(piece, weight):
        folded = piece.reshape(slots, 2 * channels, nlat)
        summed = jnp.einsum("mcl,mld->mcd", folded, legendre, preferred_element_type=jnp.float32)
        spectrum = (summed.reshape(slots, 2, channels, degrees) * damping[:, None]).reshape(
            slots, 2 * channels, degrees
        )
        spectrum = spectrum.astype(jnp.bfloat16)
        result = jnp.einsum("mcd,mld->mcl", spectrum, legendre, preferred_element_type=jnp.float32)
        if weight is not None:
            result = result * weight[None, None, :]
        return result.astype(jnp.bfloat16).reshape(2 * slots, channels, nlat)

    state_coef = (analysis(state_field) * quad_rows[None, None, :]).astype(jnp.bfloat16)
    state_waves = lax.all_to_all(state_coef, "band", split_axis=0, concat_axis=2, tiled=True)
    state_back = legendre_pass(state_waves, None)
    state_lines = lax.all_to_all(state_back, "band", split_axis=2, concat_axis=0, tiled=True)
    grid_state = synthesis(state_lines).astype(jnp.bfloat16).reshape(channels, lat_dev * NLON)
    cot_grid = cotangent[0]

    def column_step(row_index, carry):
        grad_in, grad_out, grad_bias, backward = carry
        start = row_index * NLON
        y_cols = lax.dynamic_slice_in_dim(grid_state, start, NLON, 1)
        g_cols = lax.dynamic_slice_in_dim(cot_grid, start, NLON, 1)
        hidden_pre = (
            lax.dot_general(
                w_in, y_cols, (((0,), (0,)), ((), ())), preferred_element_type=jnp.float32
            )
            + b_in[:, None]
        )
        sigma = jax.nn.sigmoid(hidden_pre)
        hidden = (hidden_pre * sigma).astype(jnp.bfloat16)
        hidden_grad = lax.dot_general(
            w_out, g_cols, (((0,), (0,)), ((), ())), preferred_element_type=jnp.float32
        )
        pre_grad = (hidden_grad * sigma * (1.0 + hidden_pre * (1.0 - sigma))).astype(jnp.bfloat16)
        grad_out = grad_out + lax.dot_general(
            g_cols, hidden, (((1,), (1,)), ((), ())), preferred_element_type=jnp.float32
        )
        grad_in = grad_in + lax.dot_general(
            y_cols, pre_grad, (((1,), (1,)), ((), ())), preferred_element_type=jnp.float32
        )
        grad_bias = grad_bias + jnp.sum(pre_grad.astype(jnp.float32), axis=1)
        back_cols = lax.dot_general(
            w_in, pre_grad, (((1,), (0,)), ((), ())), preferred_element_type=jnp.float32
        ).astype(jnp.bfloat16)
        backward = lax.dynamic_update_slice_in_dim(backward, back_cols, start, 1)
        return (grad_in, grad_out, grad_bias, backward)

    hidden_units = w_in.shape[1]
    initial = (
        jnp.zeros((channels, hidden_units), jnp.float32),
        jnp.zeros((channels, hidden_units), jnp.float32),
        jnp.zeros((hidden_units,), jnp.float32),
        jnp.zeros((channels, lat_dev * NLON), jnp.bfloat16),
    )
    grad_in, grad_out, grad_bias, back_grid = lax.fori_loop(0, lat_dev, column_step, initial)
    members = state.shape[0] * lax.axis_size("ens")
    scale = 1.0 / math.sqrt(members * nlat * NLON)
    grad_in, grad_out, grad_bias = lax.psum(
        (grad_in * scale, grad_out * scale, grad_bias * scale), ("band", "ens")
    )
    physics_coef = analysis(back_grid.reshape(channels, lat_dev, NLON)).astype(jnp.bfloat16)
    direct_coef = analysis(cot_field).astype(jnp.bfloat16)
    direct_waves, physics_waves = (
        lax.all_to_all(direct_coef, "band", split_axis=0, concat_axis=2, tiled=True),
        lax.all_to_all(physics_coef, "band", split_axis=0, concat_axis=2, tiled=True),
    )
    adjoint_waves = add_coefs(direct_waves, physics_waves)
    adjoint_back = legendre_pass(adjoint_waves, quad)
    adjoint_lines = lax.all_to_all(adjoint_back, "band", split_axis=2, concat_axis=0, tiled=True)
    state_grad = synthesis(adjoint_lines).astype(jnp.bfloat16).reshape(1, channels, lat_dev * NLON)
    return (state_grad, grad_in, grad_out, grad_bias)


def solution(mesh):
    placed = (
        P("ens", None, "band"),
        P("ens", None, "band"),
        P(),
        P(),
        P(),
        P("band", None, None),
        P(),
        P(),
        P(),
    )
    return jax.shard_map(
        body,
        mesh=mesh,
        in_specs=placed,
        out_specs=(P("ens", None, "band"), P(), P(), P()),
        check_vma=False,
    )
```

profile of v0, /device:TPU:1, one launch (start us, length us, event | category | flops | bytes accessed | tf_op | source)
XLA Modules:
  0.0 745.1 jit_solution(13311440491131187431)
XLA Ops:
  8.1 6.1 fusion.31
  14.6 3.3 copy.75
  17.8 3.6 convert_element_type.131
  21.5 4.5 reshape_squeeze.7
  27.9 2.1 copy.82
  30.1 19.3 %all-to-all-start.1 = ((bf16[512,114,4]{1,2,0:T(4,128)(2,1)}), bf16[512,114,4]{1,2,0:T(4,128)(2,1)S(1)}, u32[]{:S(2)}, u32[]{:S(2)}) async-start(bf16[512,114,4]{1,2,0:T(4,128)(2,1)} %copy.82), calls=%async_computation.1 | async-start | bytes 1048576 | tf_op jit(solution)/shard_map/all_to_all | solution.py:68
  50.6 28.1 %all-to-all-done.1 = bf16[512,114,4]{1,2,0:T(4,128)(2,1)S(1)} async-done(((bf16[512,114,4]{1,2,0:T(4,128)(2,1)}), bf16[512,114,4]{1,2,0:T(4,128)(2,1)S(1)}, u32[]{:S(2)}, u32[]{:S(2)}) %all-to-all-start.1) | async-done | bytes 466976 | tf_op jit(solution)/shard_map/all_to_all | solution.py:68
  84.0 8.6 %all-to-all-start.2 = ((bf16[8,114,256]{1,0,2:T(8,128)(2,1)}), bf16[8,114,256]{1,0,2:T(8,128)(2,1)S(1)}, u32[]{:S(2)}, u32[]{:S(2)}) async-start(bf16[8,114,256]{1,0,2:T(8,128)(2,1)} %copy.87), calls=%async_computation.2 | async-start | bytes 1048576 | tf_op jit(solution)/shard_map/all_to_all | solution.py:70
  92.7 4.8 reshape_squeeze.6
  97.5 2.3 fusion.38
  100.9 20.8 %all-to-all-done.2 = bf16[8,114,256]{1,0,2:T(8,128)(2,1)S(1)} async-done(((bf16[8,114,256]{1,0,2:T(8,128)(2,1)}), bf16[8,114,256]{1,0,2:T(8,128)(2,1)S(1)}, u32[]{:S(2)}, u32[]{:S(2)}) %all-to-all-start.2) | async-done | bytes 466976 | tf_op jit(solution)/shard_map/all_to_all | solution.py:70
  121.8 9.4 %all-to-all-start = ((bf16[512,114,4]{1,2,0:T(4,128)(2,1)}), bf16[512,114,4]{1,2,0:T(4,128)(2,1)}, u32[]{:S(2)}, u32[]{:S(2)}) async-start(bf16[512,114,4]{1,2,0:T(4,128)(2,1)} %copy.78), calls=%async_computation | async-start | bytes 1048576 | tf_op jit(solution)/shard_map/all_to_all | solution.py:120
  131.1 2.1 convolution_convert_fusion.2
  136.3 60.7 %while.20 = (s32[]{:T(128)}, f32[114,384]{1,0:T(8,128)}, f32[114,384]{1,0:T(8,128)}, f32[384]{0:T(512)S(1)}, bf16[114,5760]{1,0:T(8,128)(2,1)}, /*index=5*/bf16[...) while((s32[]{:T(128)}, f32[114,384]{1,0:T(8,128)}, ...), condition=%wide.region_2.3_spmd.clone, body=%wide.region_0.2_spmd.clone.sunk | while | flops 640114368 | bytes 22245492 | solution.py:111
  137.7 2.7 convert_reduce_fusion.2
  141.4 3.3 convolution_add_fusion.6
  146.2 4.4 dynamic_update_slice.9
  151.9 2.7 convert_reduce_fusion.2
  156.7 3.3 convolution_add_fusion.6
  161.4 4.9 dynamic_update_slice.9
  167.6 2.7 convert_reduce_fusion.2
  172.3 3.3 convolution_add_fusion.6
  177.1 4.9 dynamic_update_slice.9
  183.3 2.6 convert_reduce_fusion.2
  188.0 3.2 convolution_add_fusion.6
  192.7 4.3 dynamic_update_slice.9
  197.6 4.2 reshape.236
  205.0 42.0 %all_to_all.69 = bf16[512,114,4]{1,2,0:T(4,128)(2,1)S(1)} all-to-all(bf16[512,114,4]{1,2,0:T(4,128)(2,1)S(1)} %copy.95), channel_id=1, replica_groups=mesh['band'=64,'ens'=8] {'band'}, dimensions={0} | all-to-all | bytes 933888 | tf_op jit(solution)/shard_map/all_to_all | solution.py:121
  252.2 10.0 %all-to-all-start.4 = ((bf16[8,114,256]{1,0,2:T(8,128)(2,1)}), bf16[8,114,256]{1,0,2:T(8,128)(2,1)S(1)}, u32[]{:S(2)}, u32[]{:S(2)}) async-start(bf16[8,114,256]{1,0,2:T(8,128)(2,1)} %copy.100), calls=%async_computation.4 | async-start | bytes 1048576 | tf_op jit(solution)/shard_map/all_to_all | solution.py:125
  264.1 106.3 %psum.23 = f32[384]{0:T(512)} all-reduce(f32[384]{0:T(512)S(1)} %broadcast_multiply_fusion.2), channel_id=1, replica_groups=mesh['band'=64,'ens'=8] {'band','ens'}, use_global_device_ids=true, to_apply=%region_5.6 | all-reduce | flops 384 | bytes 3072 | tf_op jit(solution)/shard_map/psum | solution.py:114
  374.4 2.3 copy.105
  376.6 358.4 %all-reduce.3.cloned.1.call-done = (f32[114,384]{1,0:T(8,128)}, f32[114,384]{1,0:T(8,128)}) async-done(((f32[114,384]{1,0:T(8,128)}, f32[114,384]{1,0:T(8,128)}), (f32[114,384]{1,0:T(8,128)}, f32[114,384]{1,0:T(8,128)})) %all-reduce.3.cloned.1.call-update) | async-done | bytes 350224 | tf_op jit(solution)/shard_map/psum | solution.py:114
  (87 shorter events, 50.2 us)
Async XLA Ops:
  7.2 73.3 %copy-start = (bf16[4,256,256]{2,1,0:T(8,128)(2,1)S(1)}, bf16[4,256,256]{2,1,0:T(8,128)(2,1)}, u32[]{:S(2)}) copy-start(bf16[4,256,256]{2,1,0:T(8,128)(2,1)} %param.16) | copy-start | bytes 1572868
  21.5 109.6 %copy-start.2 = (bf16[512,1440]{1,0:T(8,128)(2,1)}, bf16[512,1440]{1,0:T(8,128)(2,1)S(1)}, u32[]{:S(2)}) copy-start(bf16[512,1440]{1,0:T(8,128)(2,1)S(1)} %convert_element_type.131) | copy-start | bytes 4423684
  21.5 4.6 copy-start.10
  27.9 21.4 %copy-start.9 = (s32[64,4]{0,1:T(4,128)S(1)}, s32[64,4]{0,1:T(4,128)}, u32[]{:S(2)}) copy-start(s32[64,4]{0,1:T(4,128)} %param.19) | copy-start | bytes 3076
  27.9 21.7 %copy-start.11 = (f32[114]{0:T(128)S(1)}, f32[114]{0:T(128)}, u32[]{:S(2)}) copy-start(f32[114]{0:T(128)} %param.17) | copy-start | bytes 1372
  30.1 48.7 %all-to-all-start.1 = ((bf16[512,114,4]{1,2,0:T(4,128)(2,1)}), bf16[512,114,4]{1,2,0:T(4,128)(2,1)S(1)}, u32[]{:S(2)}, u32[]{:S(2)}) async-start(bf16[512,114,4]{1,2,0:T(4,128)(2,1)} %copy.82), calls=%async_computation.1 | async-start | bytes 1048576 | tf_op jit(solution)/shard_map/all_to_all | solution.py:68
  80.5 1.3 copy-start.4
  84.0 37.8 %all-to-all-start.2 = ((bf16[8,114,256]{1,0,2:T(8,128)(2,1)}), bf16[8,114,256]{1,0,2:T(8,128)(2,1)S(1)}, u32[]{:S(2)}, u32[]{:S(2)}) async-start(bf16[8,114,256]{1,0,2:T(8,128)(2,1)} %copy.87), calls=%async_computation.2 | async-start | bytes 1048576 | tf_op jit(solution)/shard_map/all_to_all | solution.py:70
  121.8 83.2 %all-to-all-start = ((bf16[512,114,4]{1,2,0:T(4,128)(2,1)}), bf16[512,114,4]{1,2,0:T(4,128)(2,1)}, u32[]{:S(2)}, u32[]{:S(2)}) async-start(bf16[512,114,4]{1,2,0:T(4,128)(2,1)} %copy.78), calls=%async_computation | async-start | bytes 1048576 | tf_op jit(solution)/shard_map/all_to_all | solution.py:120
  133.2 3.1 copy-start.8
  137.6 2.7 copy-start.1
  151.9 2.7 copy-start.1
  167.6 2.7 copy-start.1
  183.3 2.6 copy-start.1
  197.0 0.6 copy-start.6
  197.6 4.2 copy-start.3
  247.0 2.5 copy-start.5
  251.1 13.0 %copy-start.7 = (f32[384]{0:T(512)S(1)}, f32[384]{0:T(512)}, u32[]{:S(2)}) copy-start(f32[384]{0:T(512)} %copy-done.6) | copy-start | bytes 4612
  252.2 118.2 %all-to-all-start.4 = ((bf16[8,114,256]{1,0,2:T(8,128)(2,1)}), bf16[8,114,256]{1,0,2:T(8,128)(2,1)S(1)}, u32[]{:S(2)}, u32[]{:S(2)}) async-start(bf16[8,114,256]{1,0,2:T(8,128)(2,1)} %copy.100), calls=%async_computation.4 | async-start | bytes 1048576 | tf_op jit(solution)/shard_map/all_to_all | solution.py:125
  262.2 472.9 %all-reduce.3.cloned.1.call-start = ((), (), s32[]{:S(2)}) async-start(), calls=%async_computation.5 | async-start | bytes 737280 | tf_op jit(solution)/shard_map/psum | solution.py:114
Sparse Core Ops, SparseCore 0:
  269.1 465.9 all-reduce.2
where the time goes:
time: 748 us; the launch traced here: 745 us
  waiting for transfers between devices  407 us (54%)
  blocking collectives  148 us (20%)
  local copies, waits for them, and re-layouts  62.3 us (8%)
  matrix products  54.8 us (7%)
  starting transfers between devices  47.3 us (6%)
  between operations  14.3 us (2%)
  other arithmetic  10.6 us (1%)
    psum x1, waiting for transfers between devices, body(): lax.psum((grad_in * scale, grad_out * scale, grad_bias * scale), ('band',...  358 us
    psum x1, blocking collectives, body(): lax.psum((grad_in * scale, grad_out * scale, grad_bias * scale), ('band',...  106 us
    all_to_all x1, blocking collectives, body(): lax.all_to_all(physics_coef, 'band', split_axis=0, concat_axis=2, tiled=T...  42 us
    all_to_all x1, waiting for transfers between devices, body(): lax.all_to_all(state_coef, 'band', split_axis=0, concat_axis=2, tiled=True)  28.1 us
    all_to_all x1, waiting for transfers between devices, body(): lax.all_to_all(state_back, 'band', split_axis=2, concat_axis=0, tiled=True)  20.8 us
    all_to_all x1, starting transfers between devices, body(): lax.all_to_all(state_coef, 'band', split_axis=0, concat_axis=2, tiled=True)  19.3 us
    dynamic_update_slice x4, local copies, waits for them, and re-layouts, column_step(): backward = lax.dynamic_update_slice_in_dim(backward, back_cols, start, 1)  18.5 us
  transfers between devices with their start and end apart: 5, of which 3 were waited for; matrix products, arithmetic and copies ran while one was open for 12% of the time, Pallas kernels for 0%

commit v1 on v0

v1 whole, which is shorter than its diff:
```python
import functools
import math

import jax
import jax.numpy as jnp
import numpy as np
from jax import lax
from jax.experimental import pallas as pl
from jax.experimental.pallas import tpu as pltpu
from jax.sharding import PartitionSpec as P

MESH = pl.DeviceIdType.MESH
F32, BF16 = jnp.float32, jnp.bfloat16
NLON = 1440
LATS = 4
LANES = 128
STEP = 11 * LANES
WINDOW = 12 * LANES
CHUNK = 5 * LANES
BLOCK = 16


def trig_table(modes):
    phase = np.outer(np.arange(modes), np.arange(NLON)) % NLON
    angle = phase.astype(np.float64) * (2.0 * math.pi / NLON)
    both = np.stack([np.cos(angle), np.sin(angle)]) / math.sqrt(NLON)
    out = np.zeros((LATS, 2, modes, WINDOW), np.float32)
    for a in range(LATS):
        shift = a * (NLON - STEP)
        out[a, :, :, shift : shift + NLON] = both
    return out.astype(jnp.bfloat16)


def nn(a, b):
    return jnp.dot(a, b, preferred_element_type=F32)


def nt(a, b):
    return lax.dot_general(a, b, (((1,), (1,)), ((), ())), preferred_element_type=F32)


def kernel(
    nx, nz, ne, scale,
    state_hbm, cot_hbm, leg_hbm, trig_hbm, w_in, w_out, bias, diffusion, quad, quad_row, table, table_v,
    grad_hbm, w_in_grad, w_out_grad, b_grad,
    state_raw, cot_raw, leg, trig, wave, state_pad, cot_pad, leg_t, w_in_pad, w_in_t, w_out_t, b_cols, damp,
    quad_cols, hidden_grad, direct, stage, stage_out, back_t, y, hidden, pre_grad, back_grid, out_v, small,
    send, recv, gt, rs1, red1, rs2, zsend, zrecv, agx, full,
    in_sem, out_sem, send_sem, recv_sem, g_send, g_recv, z_send, z_recv,
):
    nb = nx * nz
    me = lax.axis_index("band")
    ens = lax.axis_index("ens")
    my_x, my_z = me // nz, lax.rem(me, nz)
    channels = state_raw.shape[0]
    hid = w_in.shape[1]
    nlat = nb * LATS
    whole = channels // 16 * 16
    cols = state_raw.shape[1]

    loads = [
        pltpu.make_async_copy(trig_hbm, trig, in_sem.at[0]),
        pltpu.make_async_copy(state_hbm.at[0], state_raw, in_sem.at[1]),
        pltpu.make_async_copy(cot_hbm.at[0], cot_raw, in_sem.at[2]),
        pltpu.make_async_copy(leg_hbm, leg, in_sem.at[3]),
    ]
    for load in loads:
        load.start()

    def peer_of(i):
        j, dx = i // nx, lax.rem(i, nx)
        up = (j + 1) // 2
        dz = jnp.where(lax.rem(j, 2) == 1, up, nz - up)
        return lax.rem(my_x + dx, nx) * nz + lax.rem(my_z + dz, nz)

    barrier = pltpu.get_barrier_semaphore()

    def greet_band(i, _):
        pl.semaphore_signal(barrier, inc=1, device_id=(peer_of(i), ens), device_id_type=MESH)
        return 0

    def greet_ens(i, _):
        pl.semaphore_signal(barrier, inc=1, device_id=(me, lax.rem(ens + i, ne)), device_id_type=MESH)
        return 0

    lax.fori_loop(1, nb, greet_band, 0)
    lax.fori_loop(1, ne, greet_ens, 0)

    def exchange(n):
        recv[n, pl.ds(me, 1)] = send[n, pl.ds(me, 1)]

        def one(i, _):
            peer = peer_of(nb - i)
            pltpu.make_async_remote_copy(
                src_ref=send.at[n, peer],
                dst_ref=recv.at[n, me],
                send_sem=send_sem.at[n],
                recv_sem=recv_sem.at[n],
                device_id=(peer, ens),
                device_id_type=MESH,
            ).start()
            return 0

        lax.fori_loop(1, nb, one, 0)

    def arrived(n):
        part = recv.at[n, pl.ds(0, nb - 1)]
        pltpu.make_async_copy(part, part, recv_sem.at[n]).wait()

    def left(n):
        part = send.at[n, pl.ds(0, nb - 1)]
        pltpu.make_async_copy(part, part, send_sem.at[n]).wait()

    def pad_rows(dst, src):
        dst[pl.ds(0, whole), :] = src[pl.ds(0, whole), :]
        dst[pl.ds(whole, 16), :] = jnp.zeros((16, dst.shape[1]), dst.dtype)
        dst[pl.ds(whole, channels - whole), :] = src[pl.ds(whole, channels - whole), :]

    def window(a):
        return pl.ds(a * STEP, WINDOW)

    modes = nb * LATS
    lane = lax.broadcasted_iota(jnp.int32, (nb, modes), 1)
    pick = jnp.concatenate(
        [(table_v[:, pl.ds(s, 1)] == lane).astype(F32) for s in range(LATS)], axis=0
    ).astype(BF16)
    loads[0].wait()
    for a in range(LATS):
        for r in range(2):
            rows = nn(pick, trig[a, r]).astype(BF16)
            for s in range(LATS):
                wave[a, pl.ds((2 * s + r) * nb, nb), :] = rows[s * nb : (s + 1) * nb]
    half = 4 * nb

    loads[1].wait()
    pad_rows(state_pad, state_raw)
    for h in range(2):
        for a in range(LATS):
            coef = nt(wave[a, pl.ds(h * half, half), :], state_pad[:, window(a)]) * quad[me * LATS + a]
            for j in range(4):
                stage[pl.ds(a * 4 + j, nb, stride=BLOCK), :] = coef[j * nb : (j + 1) * nb]
        send[h] = stage[pl.ds(0, nb * BLOCK), :].reshape(nb, BLOCK, LANES).astype(BF16)
        if h == 0:
            pl.semaphore_wait(barrier, nb - 1 + ne - 1)
        exchange(h)

    loads[3].wait()
    for s in range(LATS):
        leg_t[s] = leg[s].astype(F32).T.astype(BF16)
    small[...] = jnp.zeros_like(small)
    small[pl.ds(0, 1), pl.ds(0, channels)] = diffusion[...]
    degree = lax.broadcasted_iota(jnp.int32, (nlat, LANES), 0)
    degree_f = degree.astype(F32)
    scaled = degree_f * (degree_f + 1.0) / (nlat * (nlat - 1.0))
    damp[...] = 1.0 / (1.0 + small[pl.ds(0, 1), :] * (scaled * scaled))
    quad_cols[...] = jnp.broadcast_to(quad_row[...], (LANES, nlat)).T
    b_cols[...] = jnp.broadcast_to(bias[...], (LANES, hid)).T
    pad_rows(w_in_pad, w_out)
    w_out_t[...] = w_in_pad[...].astype(F32).T.astype(BF16)
    pad_rows(w_in_pad, w_in)
    w_in_t[...] = w_in_pad[...].astype(F32).T.astype(BF16)
    loads[2].wait()
    pad_rows(cot_pad, cot_raw)
    for a in range(LATS):
        direct[a] = nt(wave[a], cot_pad[:, window(a)])

    def weigh(i, _):
        at = pl.ds(pl.multiple_of(i * CHUNK, LANES), CHUNK)
        hidden_grad[:, at] = nn(w_out_t[...], cot_pad[:, at])
        return 0

    lax.fori_loop(0, cols // CHUNK, weigh, 0)

    def legendre_half(n, h, offset, stride, weight):
        for sub in range(2):
            s = 2 * h + sub
            lines = jnp.concatenate(
                [stage[pl.ds(offset + 2 * sub + r, nlat, stride=stride), :] for r in range(2)], axis=1
            ).astype(BF16)
            keep = jnp.where(degree >= table[me, s], damp[...], 0.0)
            spectrum = (nn(leg_t[s], lines) * jnp.concatenate([keep, keep], axis=1)).astype(BF16)
            back = nn(leg[s], spectrum)
            for r in range(2):
                part = back[:, r * LANES : (r + 1) * LANES]
                if weight:
                    part = part * quad_cols[...]
                stage_out[pl.ds(2 * sub + r, nlat, stride=4), :] = part
        send[n] = stage_out[...].reshape(nb, BLOCK, LANES).astype(BF16)
        exchange(n)

    def gather_half(n, h):
        arrived(n)
        stage[pl.ds(0, nb * BLOCK), :] = recv[n].astype(F32).reshape(nb * BLOCK, LANES)
        for a in range(LATS):
            rows = jnp.concatenate(
                [stage[pl.ds(a * 4 + j, nb, stride=BLOCK), :] for j in range(4)], axis=0
            )
            back_t[a, :, pl.ds(h * half, half)] = rows.T.astype(BF16)

    def synthesis(write):
        tail = None
        for a in range(LATS):
            lines = nn(back_t[a], wave[a])
            head = lines[:, :LANES] if tail is None else lines[:, :LANES] + tail
            write(a * STEP, head)
            write(a * STEP + LANES, lines[:, LANES:STEP])
            tail = lines[:, STEP:]
        write(LATS * STEP, tail)

    for h in range(2):
        arrived(h)
        stage[pl.ds(0, nb * BLOCK), :] = recv[h].astype(F32).reshape(nb * BLOCK, LANES)
        legendre_half(2 + h, h, 0, 4, False)
    for h in range(2):
        gather_half(2 + h, h)

    def write_y(start, lines):
        row = lax.broadcasted_iota(jnp.int32, lines.shape, 0)
        lines = jnp.where(row < channels, lines, jnp.where(row == channels, 1.0, 0.0))
        y[:, pl.ds(start, lines.shape[1])] = lines.astype(BF16)

    synthesis(write_y)

    def network(i, _):
        at = pl.ds(pl.multiple_of(i * CHUNK, LANES), CHUNK)
        pre = nn(w_in_t[...], y[:, at]) + jnp.concatenate([b_cols[...]] * (CHUNK // LANES), axis=1)
        sigma = 0.5 * jnp.tanh(0.5 * pre) + 0.5
        act = pre * sigma
        grad = (hidden_grad[:, at] * (sigma + act * (1.0 - sigma))).astype(BF16)
        hidden[:, at] = act.astype(BF16)
        pre_grad[:, at] = grad
        back_grid[:, at] = nn(w_in_pad[...], grad).astype(BF16)
        return 0

    chunks = cols // CHUNK
    first = -(-(2 * NLON) // CHUNK)
    for p in range(2):
        lax.fori_loop(0 if p == 0 else first, first if p == 0 else chunks, network, 0)
        for sub in range(2):
            a = 2 * p + sub
            coef = direct[a] + nt(wave[a], back_grid[:, window(a)])
            for k in range(8):
                stage[pl.ds(sub * 8 + k, nb, stride=BLOCK), :] = coef[k * nb : (k + 1) * nb]
        send[4 + p] = stage[pl.ds(0, nb * BLOCK), :].reshape(nb, BLOCK, LANES).astype(BF16)
        exchange(4 + p)

    per_e = 2 * hid // ne
    per_x = per_e // nx
    wide = cols // 5
    gt[...] = jnp.zeros_like(gt)

    def gradients(i, _):
        at = pl.ds(pl.multiple_of(i * wide, LANES), wide)
        g_in = nt(pre_grad[:, at], y[:, at])
        g_out = nt(hidden[:, at], cot_pad[:, at])
        gt[...] += jnp.concatenate([g_in, g_out], axis=0).reshape(gt.shape)
        return 0

    lax.fori_loop(0, 5, gradients, 0)

    def to_ens(src, dst, n):
        def one(i, _):
            other = lax.rem(ens + i, ne)
            pltpu.make_async_remote_copy(
                src_ref=src(other), dst_ref=dst, send_sem=g_send.at[n], recv_sem=g_recv.at[n],
                device_id=(me, other), device_id_type=MESH,
            ).start()
            return 0

        lax.fori_loop(1, ne, one, 0)

    def to_x(src, dst, n):
        def one(i, _):
            other = lax.rem(my_x + i, nx)
            pltpu.make_async_remote_copy(
                src_ref=src(other), dst_ref=dst, send_sem=g_send.at[n], recv_sem=g_recv.at[n],
                device_id=(other * nz + my_z, ens), device_id_type=MESH,
            ).start()
            return 0

        lax.fori_loop(1, nx, one, 0)

    def took(ref, count, sem):
        part = ref.at[pl.ds(0, count)]
        pltpu.make_async_copy(part, part, sem).wait()

    rs1[pl.ds(ens, 1)] = gt[pl.ds(ens, 1)]
    to_ens(lambda other: gt.at[other], rs1.at[ens], 0)
    took(rs1, ne - 1, g_recv.at[0])
    red1[...] = jnp.sum(rs1[...], axis=0).reshape(nx, per_x, LANES)
    rs2[pl.ds(my_x, 1)] = red1[pl.ds(my_x, 1)]
    to_x(lambda other: red1.at[other], rs2.at[my_x], 1)

    for p in range(2):
        arrived(4 + p)
    lines = jnp.concatenate([recv[4].astype(F32), recv[5].astype(F32)], axis=1)
    stage[...] = lines.reshape(2 * nb * BLOCK, LANES)
    for h in range(2):
        legendre_half(6 + h, h, 4 * h, 8, True)

    took(rs2, nx - 1, g_recv.at[1])
    total = jnp.sum(rs2[...], axis=0)
    step, distance = 0, 1
    while distance < nz:
        partner = my_z + distance * (1 - 2 * lax.rem(my_z // distance, 2))
        zsend[step] = total
        copy = pltpu.make_async_remote_copy(
            src_ref=zsend.at[step], dst_ref=zrecv.at[step], send_sem=z_send.at[step],
            recv_sem=z_recv.at[step], device_id=(my_x * nz + partner, ens), device_id_type=MESH,
        )
        copy.start()
        copy.wait()
        total = total + zrecv[step]
        step, distance = step + 1, 2 * distance
    agx[pl.ds(my_x, 1)] = total[None]
    to_x(lambda other: agx.at[my_x], agx.at[my_x], 2)
    took(agx, nx - 1, g_recv.at[2])
    full[pl.ds(ens, 1)] = agx[...].reshape(1, per_e, LANES)
    to_ens(lambda other: full.at[ens], full.at[ens], 3)
    gather_half(6, 0)
    took(full, ne - 1, g_recv.at[3])
    sums = (full[...] * scale).reshape(2 * hid, LANES)
    g_in, g_out = sums[:hid].T, sums[hid:].T
    w_in_grad[...] = g_in[:channels]
    w_out_grad[...] = g_out[:channels]
    b_grad[...] = g_in[channels : channels + 1]

    gather_half(7, 1)

    def write_out(start, lines):
        out_v[:, pl.ds(start, lines.shape[1])] = lines[:channels].astype(BF16)

    synthesis(write_out)
    store = pltpu.make_async_copy(out_v, grad_hbm.at[0], out_sem)
    store.start()
    for n in range(8):
        left(n)
    took(gt, ne - 1, g_send.at[0])
    took(red1, nx - 1, g_send.at[1])
    took(agx, nx - 1, g_send.at[2])
    took(full, ne - 1, g_send.at[3])
    store.wait()


def body(nx, nz, ne, state, cotangent, w_in, b_in, w_out, legendre, diffusion, quad, table):
    nb = nx * nz
    channels, cols = state.shape[1:]
    hid = w_in.shape[1]
    nlat = legendre.shape[1]
    modes = nb * LATS
    per_e = 2 * hid // ne
    per_x = per_e // nx
    steps = max(1, nz.bit_length() - 1)
    scale = 1.0 / math.sqrt(ne * nlat * NLON)
    any_spec = pl.BlockSpec(memory_space=pl.ANY)
    vmem = pl.BlockSpec(memory_space=pltpu.VMEM)
    smem = pl.BlockSpec(memory_space=pltpu.SMEM)
    dma = pltpu.SemaphoreType.DMA
    grad, g_in, g_out, g_b = pl.pallas_call(
        functools.partial(kernel, nx, nz, ne, scale),
        out_shape=(
            jax.ShapeDtypeStruct((1, channels, cols), BF16),
            jax.ShapeDtypeStruct((channels, hid), F32),
            jax.ShapeDtypeStruct((channels, hid), F32),
            jax.ShapeDtypeStruct((1, hid), F32),
        ),
        in_specs=[any_spec] * 4 + [vmem] * 4 + [smem, vmem, smem, vmem],
        out_specs=(any_spec, vmem, vmem, vmem),
        scratch_shapes=[
            pltpu.VMEM((channels, cols), BF16),
            pltpu.VMEM((channels, cols), BF16),
            pltpu.VMEM((LATS, nlat, nlat), BF16),
            pltpu.VMEM((LATS, 2, modes, WINDOW), BF16),
            pltpu.VMEM((LATS, 2 * modes, WINDOW), BF16),
            pltpu.VMEM((LANES, cols), BF16),
            pltpu.VMEM((LANES, cols), BF16),
            pltpu.VMEM((LATS, nlat, nlat), BF16),
            pltpu.VMEM((LANES, hid), BF16),
            pltpu.VMEM((hid, LANES), BF16),
            pltpu.VMEM((hid, LANES), BF16),
            pltpu.VMEM((hid, LANES), F32),
            pltpu.VMEM((nlat, LANES), F32),
            pltpu.VMEM((nlat, LANES), F32),
            pltpu.VMEM((hid, cols), F32),
            pltpu.VMEM((LATS, 2 * modes, LANES), F32),
            pltpu.VMEM((2 * nb * BLOCK, LANES), F32),
            pltpu.VMEM((nb * BLOCK, LANES), F32),
            pltpu.VMEM((LATS, LANES, 2 * modes), BF16),
            pltpu.VMEM((LANES, cols), BF16),
            pltpu.VMEM((hid, cols), BF16),
            pltpu.VMEM((hid, cols), BF16),
            pltpu.VMEM((LANES, cols), BF16),
            pltpu.VMEM((channels, cols), BF16),
            pltpu.VMEM((8, LANES), F32),
            pltpu.VMEM((8, nb, BLOCK, LANES), BF16),
            pltpu.VMEM((8, nb, BLOCK, LANES), BF16),
            pltpu.VMEM((ne, per_e, LANES), F32),
            pltpu.VMEM((ne, per_e, LANES), F32),
            pltpu.VMEM((nx, per_x, LANES), F32),
            pltpu.VMEM((nx, per_x, LANES), F32),
            pltpu.VMEM((steps, per_x, LANES), F32),
            pltpu.VMEM((steps, per_x, LANES), F32),
            pltpu.VMEM((nx, per_x, LANES), F32),
            pltpu.VMEM((ne, per_e, LANES), F32),
            dma((4,)),
            dma,
            dma((8,)),
            dma((8,)),
            dma((4,)),
            dma((4,)),
            dma((steps,)),
            dma((steps,)),
        ],
        compiler_params=pltpu.CompilerParams(
            collective_id=0, has_side_effects=True, vmem_limit_bytes=60 * 1024 * 1024
        ),
    )(
        state, cotangent, legendre, jnp.asarray(trig_table(modes)), w_in, w_out, b_in.reshape(1, hid),
        diffusion.reshape(1, channels), quad, quad.reshape(1, nlat), table, table,
    )
    return grad, g_in, g_out, g_b.reshape(hid)


def solution(mesh):
    nb, ne = mesh.shape["band"], mesh.shape["ens"]
    nx = 4 if nb == 64 else 2
    placed = (
        P("ens", None, "band"),
        P("ens", None, "band"),
        P(),
        P(),
        P(),
        P("band", None, None),
        P(),
        P(),
        P(),
    )
    return jax.shard_map(
        functools.partial(body, nx, nb // nx, ne),
        mesh=mesh,
        in_specs=placed,
        out_specs=(P("ens", None, "band"), P(), P(), P()),
        check_vma=False,
    )
```

time: 748 us -> 159 us (0.21)
  waiting for transfers between devices: 407 us -> 0 us
  Pallas kernels: 0 us -> 150 us
  blocking collectives: 148 us -> 0 us
  local copies, waits for them, and re-layouts: 62.3 us -> 6.54 us
  matrix products: 54.8 us -> 0 us
  starting transfers between devices: 47.3 us -> 0 us
  between operations: 14.3 us -> 0.64 us
  other arithmetic: 10.6 us -> 1.28 us
    psum x1 -> x0, waiting for transfers between devices: 358 us -> none  [body(): lax.psum((grad_in * scale, grad_out * scale, grad_bias * scale), ('band',...]
    pallas_call x0 -> x1, Pallas kernels: none -> 150 us  [body(): pl.pallas_call(functools.partial(kernel, nx, nz, ne, scale), out_shape=(j...]
    psum x1 -> x0, blocking collectives: 106 us -> none  [body(): lax.psum((grad_in * scale, grad_out * scale, grad_bias * scale), ('band',...]
    dot_general x27 -> x0, matrix products: 54.8 us -> none  [the longest x4 13 us: column_step(): lax.dot_general(g_cols, hidden, (((1,), (1,)), ((), ())), preferred_eleme...]
    all_to_all x4 -> x0, waiting for transfers between devices: 49 us -> none  [the longest x1 28.1 us: body(): lax.all_to_all(state_coef, 'band', split_axis=0, concat_axis=2, tiled=True)]
    all_to_all x4 -> x0, starting transfers between devices: 47.3 us -> none  [the longest x1 19.3 us: body(): lax.all_to_all(state_coef, 'band', split_axis=0, concat_axis=2, tiled=True)]
    all_to_all x1 -> x0, blocking collectives: 42 us -> none  [body(): lax.all_to_all(physics_coef, 'band', split_axis=0, concat_axis=2, tiled=T...]
    dynamic_update_slice x4 -> x0, local copies, waits for them, and re-layouts: 18.5 us -> none  [column_step(): backward = lax.dynamic_update_slice_in_dim(backward, back_cols, start, 1)]
  transfers between devices with their start and end apart: 5 -> 0, of which waited for: 3 -> 0; matrix products, arithmetic and copies ran while one was open for 12% -> 0% of each run, Pallas kernels for 0% -> 0%
where the time goes in v1:
time: 159 us
  Pallas kernels  150 us (94%)
  local copies, waits for them, and re-layouts  6.54 us (4%)
    pallas_call x1, Pallas kernels, body(): pl.pallas_call(functools.partial(kernel, nx, nz, ne, scale), out_shape=(j...  150 us
    unnamed x8, local copies, waits for them, and re-layouts  5.3 us

profile of v1, /device:TPU:1, one launch (start us, length us, event | category | flops | bytes accessed | tf_op | source)
XLA Modules:
  0.0 158.6 jit_solution(9754425080654891461)
XLA Ops:
  0.6 1.2 reshape.20.bias
  1.9 1.4 copy.14.table.table_v
  3.3 150.1 %shard_map.129 = (bf16[1,114,5760]{2,1,0:T(8,128)(2,1)}, f32[114,384]{1,0:T(8,128)}, f32[114,384]{1,0:T(8,128)}, f32[1,384]{1,0:T(1,128)}) custom-call(bf16[1,114,5760]{2,1,0:T(8,128)(2,1)} %state_hbm.1, bf16[1,114,5760]{2,1,0:T(8,128)(2,1)} %cot_hbm.1, bf16[4,256,256]{2,1,0:T(8,128)(2,1)} %leg_hbm.1, bf16[4,2,256,1536]{3,2,1,0:T(8,128)(2,1)} %constant.2.clone.trig_hbm, ...), custom_call_target="tpu_custom_call" | custom-call | tf_op jit(solution)/shard_map/pallas_call | solution.py:359
  153.4 1.3 reduce
  154.7 0.0 copy-start.1
  154.7 0.0 copy-start
  154.7 2.6 %copy.19 = bf16[1,114,5760]{2,1,0:T(8,128)(2,1)} copy(bf16[1,114,5760]{2,1,0:T(8,128)(2,1)} %get-tuple-element.16) | data formatting | bytes 2626560
  157.2 0.0 copy-done.1
  157.2 0.7 copy.20
  157.9 0.0 copy-done
  157.9 0.7 copy.21
Async XLA Ops:
  154.7 2.6 %copy-start.1 = (f32[114,384]{1,0:T(8,128)S(1)}, f32[114,384]{1,0:T(8,128)}, u32[]{:S(2)}) copy-start(f32[114,384]{1,0:T(8,128)} %get-tuple-element.17) | copy-start | bytes 525316
  154.7 3.2 %copy-start = (f32[114,384]{1,0:T(8,128)S(1)}, f32[114,384]{1,0:T(8,128)}, u32[]{:S(2)}) copy-start(f32[114,384]{1,0:T(8,128)} %get-tuple-element.18) | copy-start | bytes 525316

commit v2 on v1

v2 whole, which is shorter than its diff:
```python
import functools
import math

import jax
import jax.numpy as jnp
import numpy as np
from jax import lax
from jax.experimental import pallas as pl
from jax.experimental.pallas import tpu as pltpu
from jax.sharding import PartitionSpec as P

MESH = pl.DeviceIdType.MESH
F32, BF16 = jnp.float32, jnp.bfloat16
NLON = 1440
LATS = 4
LANES = 128
STEP = 11 * LANES
WINDOW = 12 * LANES
CHUNK = 6 * LANES
BLOCK = 16


def trig_table(modes):
    phase = np.outer(np.arange(modes), np.arange(NLON)) % NLON
    angle = phase.astype(np.float64) * (2.0 * math.pi / NLON)
    both = np.stack([np.cos(angle), np.sin(angle)]) / math.sqrt(NLON)
    out = np.zeros((LATS, 2, modes, WINDOW), np.float32)
    for a in range(LATS):
        shift = a * (NLON - STEP)
        out[a, :, :, shift : shift + NLON] = both
    return out.astype(jnp.bfloat16)


def nn(a, b):
    return jnp.dot(a, b, preferred_element_type=F32)


def nt(a, b):
    return lax.dot_general(a, b, (((1,), (1,)), ((), ())), preferred_element_type=F32)


def kernel(
    nx, nz, ne, scale,
    state_hbm, cot_hbm, leg_hbm, trig_hbm, w_in, w_out, bias, diffusion, quad, quad_row, table, table_v,
    grad_hbm, w_in_grad, w_out_grad, b_grad,
    state_raw, cot_raw, leg_raw, trig, wave, state_pad, cot_pad, leg, leg_t, leg_f, w_in_pad, w_in_t, w_out_t, b_cols,
    keep, quad_cols, hidden_grad, direct, stage_0, stage_1, partial, back_t, tail, y, hidden, pre_grad, back_grid,
    out_v, small, picks, send, recv, gt, rs1, red1, rs2, zsend, zrecv, agx, full,
    in_sem, out_sem, send_sem, recv_sem, g_send, g_recv, z_send, z_recv,
):
    nb = nx * nz
    me = lax.axis_index("band")
    ens = lax.axis_index("ens")
    my_x, my_z = me // nz, lax.rem(me, nz)
    channels = state_raw.shape[0]
    hid = w_in.shape[1]
    nlat = nb * LATS
    modes = nb * LATS
    pair = 2 * nb
    whole = channels // 16 * 16
    cols = state_raw.shape[1]
    stage = (stage_0, stage_1)

    load_state = pltpu.make_async_copy(state_hbm.at[0], state_raw, in_sem.at[0])
    load_trig = [pltpu.make_async_copy(trig_hbm.at[a], trig.at[a], in_sem.at[1 + a]) for a in range(LATS)]
    load_cot = pltpu.make_async_copy(cot_hbm.at[0], cot_raw, in_sem.at[5])
    load_leg = pltpu.make_async_copy(leg_hbm, leg_raw, in_sem.at[6])
    for load in (load_state, *load_trig, load_cot, load_leg):
        load.start()

    def peer_of(i):
        j, dx = i // nx, lax.rem(i, nx)
        up = (j + 1) // 2
        dz = jnp.where(lax.rem(j, 2) == 1, up, nz - up)
        return lax.rem(my_x + dx, nx) * nz + lax.rem(my_z + dz, nz)

    barrier = pltpu.get_barrier_semaphore()

    def greet_band(i, _):
        pl.semaphore_signal(barrier, inc=1, device_id=(peer_of(i), ens), device_id_type=MESH)
        return 0

    def greet_ens(i, _):
        pl.semaphore_signal(barrier, inc=1, device_id=(me, lax.rem(ens + i, ne)), device_id_type=MESH)
        return 0

    lax.fori_loop(1, nb, greet_band, 0)
    lax.fori_loop(1, ne, greet_ens, 0)

    def exchange(n, p):
        send[n] = stage[p][...].reshape(nb, BLOCK, LANES).astype(BF16)
        recv[n, pl.ds(me, 1)] = send[n, pl.ds(me, 1)]
        if n == 0:
            pl.semaphore_wait(barrier, nb - 1 + ne - 1)

        def one(i, _):
            peer = peer_of(nb - i)
            pltpu.make_async_remote_copy(
                src_ref=send.at[n, peer],
                dst_ref=recv.at[n, me],
                send_sem=send_sem.at[n],
                recv_sem=recv_sem.at[n],
                device_id=(peer, ens),
                device_id_type=MESH,
            ).start()
            return 0

        lax.fori_loop(1, nb, one, 0)

    def arrived(n, p):
        part = recv.at[n, pl.ds(0, nb - 1)]
        pltpu.make_async_copy(part, part, recv_sem.at[n]).wait()
        stage[p][...] = recv[n].astype(F32).reshape(nb * BLOCK, LANES)

    def left(n):
        part = send.at[n, pl.ds(0, nb - 1)]
        pltpu.make_async_copy(part, part, send_sem.at[n]).wait()

    def rows_of(sub, k):
        return pl.ds(sub * 8 + k, nb, stride=BLOCK)

    def pad_rows(dst, src, at):
        dst[pl.ds(0, whole), at] = src[pl.ds(0, whole), at]
        dst[pl.ds(whole, 16), at] = jnp.zeros((16, at.size), dst.dtype)
        dst[pl.ds(whole, channels - whole), at] = src[pl.ds(whole, channels - whole), at]

    def window(a):
        return pl.ds(a * STEP, WINDOW)

    small[...] = jnp.zeros_like(small)
    small[pl.ds(0, LATS), pl.ds(0, nb)] = table_v[...].astype(F32)
    turned = small[...].T
    lane = lax.broadcasted_iota(jnp.int32, (nb, modes), 1).astype(F32)
    picks[...] = jnp.concatenate(
        [(turned[:nb, s : s + 1] == lane).astype(F32) for s in range(LATS)], axis=0
    ).astype(BF16)

    load_state.wait()
    for p in range(2):
        pad_rows(state_pad, state_raw, pl.ds(p * 2 * STEP, cols - 2 * STEP if p else 2 * STEP + LANES))
        pieces = []
        for sub in range(2):
            a = 2 * p + sub
            load_trig[a].wait()
            coef = nt(trig[a].reshape(2 * modes, WINDOW), state_pad[:, window(a)])
            coef = (coef * quad[me * LATS + a]).astype(BF16)
            pieces += [coef[:modes], coef[modes:]]
        picked = nn(picks[...], jnp.concatenate(pieces, axis=1))
        for sub in range(2):
            for k in range(8):
                s, r = k // 2, k % 2
                at = (2 * sub + r) * LANES
                stage[p][rows_of(sub, k), :] = picked[s * nb : (s + 1) * nb, at : at + LANES]
        exchange(p, p)

    for a in range(LATS):
        for r in range(2):
            rows = nn(picks[...], trig[a, r]).astype(BF16)
            for s in range(LATS):
                wave[a, pl.ds((2 * s + r) * nb, nb), :] = rows[s * nb : (s + 1) * nb]
    load_leg.wait()
    for s in range(LATS):
        sides = []
        for side in range(leg_f.shape[0]):
            side_cols = pl.ds(side * leg_f.shape[2], leg_f.shape[2])
            leg_f[side] = leg_raw[s, :, side_cols].astype(F32)
            sides.append(
                jnp.concatenate([leg_f[side, pl.ds(a, nb, stride=LATS), :] for a in range(LATS)], axis=0)
            )
        ordered = jnp.concatenate(sides, axis=1)
        leg[s] = ordered.astype(BF16)
        leg_t[s] = ordered.T.astype(BF16)
    small[pl.ds(0, 1), :] = jnp.zeros((1, LANES), F32)
    small[pl.ds(0, 1), pl.ds(0, channels)] = diffusion[...]
    degree = lax.broadcasted_iota(jnp.int32, (nlat, LANES), 0)
    degree_f = degree.astype(F32)
    scaled = degree_f * (degree_f + 1.0) / (nlat * (nlat - 1.0))
    damp = 1.0 / (1.0 + small[pl.ds(0, 1), :] * (scaled * scaled))
    for s in range(LATS):
        kept = jnp.where(degree >= table[s, me], damp, 0.0)
        keep[s] = jnp.concatenate([kept, kept], axis=1)
    stage_quad = jnp.broadcast_to(quad_row[...], (LANES, nlat)).T
    quad_cols[0] = stage_quad
    for a in range(LATS):
        quad_cols[1, pl.ds(a * nb, nb), :] = quad_cols[0, pl.ds(a, nb, stride=LATS), :]
    b_cols[...] = jnp.broadcast_to(bias[...].reshape(1, hid), (LANES, hid)).T
    pad_rows(w_in_pad, w_out, pl.ds(0, hid))
    w_out_t[...] = w_in_pad[...].astype(F32).T.astype(BF16)
    pad_rows(w_in_pad, w_in, pl.ds(0, hid))
    w_in_t[...] = w_in_pad[...].astype(F32).T.astype(BF16)
    load_cot.wait()
    pad_rows(cot_pad, cot_raw, pl.ds(0, cols))
    for a in range(LATS):
        direct[a] = nt(wave[a], cot_pad[:, window(a)])
    wide = cols // 5

    def weigh(i, _):
        at = pl.ds(pl.multiple_of(i * wide, LANES), wide)
        hidden_grad[:, at] = nn(w_out_t[...], cot_pad[:, at])
        return 0

    lax.fori_loop(0, 5, weigh, 0)

    def legendre(n, weight):
        def lines(p, s):
            parts = [
                jnp.concatenate([stage[p][rows_of(sub, 2 * s + r), :] for sub in range(2)], axis=0)
                for r in range(2)
            ]
            return jnp.concatenate(parts, axis=1).astype(BF16)

        arrived(n, 0)
        for s in range(LATS):
            partial[s] = nn(leg_t[s, :, pl.ds(0, pair)], lines(0, s))
        arrived(n + 1, 1)
        spectrum = []
        for s in range(LATS):
            summed = partial[s] + nn(leg_t[s, :, pl.ds(pair, pair)], lines(1, s))
            spectrum.append((summed * keep[s]).astype(BF16))
        for p in range(2):
            for s in range(LATS):
                back = nn(leg[s, pl.ds(p * pair, pair), :], spectrum[s])
                for r in range(2):
                    part = back[:, r * LANES : (r + 1) * LANES]
                    if weight:
                        part = part * quad_cols[1, pl.ds(p * pair, pair), :]
                    for sub in range(2):
                        stage[p][rows_of(sub, 2 * s + r), :] = part[sub * nb : (sub + 1) * nb]
            exchange(n + 2 + p, p)

    def synthesis(n, p, write):
        arrived(n, p)
        for sub in range(2):
            rows = jnp.concatenate([stage[p][rows_of(sub, k), :] for k in range(8)], axis=0)
            back_t[sub] = rows.T.astype(BF16)
        held = tail[...] if p else None
        for sub in range(2):
            a = 2 * p + sub
            lines = nn(back_t[sub], wave[a])
            write(a * STEP, lines[:, :LANES] if held is None else lines[:, :LANES] + held)
            write(a * STEP + LANES, lines[:, LANES:STEP])
            held = lines[:, STEP:]
        if p == 0:
            tail[...] = held
        write((2 * p + 2) * STEP, held)

    legendre(0, False)

    def write_y(start, lines):
        row = lax.broadcasted_iota(jnp.int32, lines.shape, 0)
        lines = jnp.where(row < channels, lines, jnp.where(row == channels, 1.0, 0.0))
        y[:, pl.ds(start, lines.shape[1])] = lines.astype(BF16)

    def network(i, _):
        at = pl.ds(pl.multiple_of(i * LANES, LANES), CHUNK)
        pre = nn(w_in_t[...], y[:, at]) + jnp.concatenate([b_cols[...]] * (CHUNK // LANES), axis=1)
        sigma = 0.5 * jnp.tanh(0.5 * pre) + 0.5
        act = pre * sigma
        grad = (hidden_grad[:, at] * (sigma + act * (1.0 - sigma))).astype(BF16)
        hidden[:, at] = act.astype(BF16)
        pre_grad[:, at] = grad
        back_grid[:, at] = nn(w_in_pad[...], grad).astype(BF16)
        return 0

    y[:, pl.ds(2 * STEP + LANES, LANES)] = jnp.zeros((LANES, LANES), BF16)
    tiles = cols // LANES
    per_pair, per_chunk = (tiles + 1) // 2, CHUNK // LANES
    trips = -(-per_pair // per_chunk)
    for p in range(2):
        synthesis(2 + p, p, write_y)
        begin = (tiles - trips * per_chunk) if p else 0
        lax.fori_loop(0, trips, lambda i, c, begin=begin: network(begin + i * per_chunk, c), 0)
        for sub in range(2):
            a = 2 * p + sub
            coef = direct[a] + nt(wave[a], back_grid[:, window(a)])
            for k in range(8):
                stage[p][rows_of(sub, k), :] = coef[k * nb : (k + 1) * nb]
        exchange(4 + p, p)

    per_e = 2 * hid // ne
    per_x = per_e // nx
    gt[...] = jnp.zeros_like(gt)

    def gradients(i, _):
        at = pl.ds(pl.multiple_of(i * wide, LANES), wide)
        g_in = nt(pre_grad[:, at], y[:, at])
        g_out = nt(hidden[:, at], cot_pad[:, at])
        gt[...] += jnp.concatenate([g_in, g_out], axis=0).reshape(gt.shape)
        return 0

    lax.fori_loop(0, 5, gradients, 0)

    def to_ens(src, dst, n):
        def one(i, _):
            other = lax.rem(ens + i, ne)
            pltpu.make_async_remote_copy(
                src_ref=src(other), dst_ref=dst, send_sem=g_send.at[n], recv_sem=g_recv.at[n],
                device_id=(me, other), device_id_type=MESH,
            ).start()
            return 0

        lax.fori_loop(1, ne, one, 0)

    def to_x(src, dst, n):
        def one(i, _):
            other = lax.rem(my_x + i, nx)
            pltpu.make_async_remote_copy(
                src_ref=src(other), dst_ref=dst, send_sem=g_send.at[n], recv_sem=g_recv.at[n],
                device_id=(other * nz + my_z, ens), device_id_type=MESH,
            ).start()
            return 0

        lax.fori_loop(1, nx, one, 0)

    def to_z(step):
        distance = 1 << step
        partner = my_z + distance * (1 - 2 * lax.rem(my_z // distance, 2))
        return pltpu.make_async_remote_copy(
            src_ref=zsend.at[step], dst_ref=zrecv.at[step], send_sem=z_send.at[step],
            recv_sem=z_recv.at[step], device_id=(my_x * nz + partner, ens), device_id_type=MESH,
        )

    def took(ref, count, sem):
        part = ref.at[pl.ds(0, count)]
        pltpu.make_async_copy(part, part, sem).wait()

    rs1[pl.ds(ens, 1)] = gt[pl.ds(ens, 1)]
    to_ens(lambda other: gt.at[other], rs1.at[ens], 0)
    took(rs1, ne - 1, g_recv.at[0])
    red1[...] = jnp.sum(rs1[...], axis=0).reshape(nx, per_x, LANES)
    rs2[pl.ds(my_x, 1)] = red1[pl.ds(my_x, 1)]
    to_x(lambda other: red1.at[other], rs2.at[my_x], 1)
    took(rs2, nx - 1, g_recv.at[1])
    zsend[0] = jnp.sum(rs2[...], axis=0)
    to_z(0).start()

    legendre(4, True)

    steps = nz.bit_length() - 1
    for step in range(steps):
        to_z(step).wait()
        total = zsend[step] + zrecv[step]
        if step + 1 < steps:
            zsend[step + 1] = total
            to_z(step + 1).start()
    agx[pl.ds(my_x, 1)] = total[None]
    to_x(lambda other: agx.at[my_x], agx.at[my_x], 2)
    took(agx, nx - 1, g_recv.at[2])
    full[pl.ds(ens, 1)] = agx[...].reshape(1, per_e, LANES)
    to_ens(lambda other: full.at[ens], full.at[ens], 3)

    def write_out(start, lines):
        out_v[:, pl.ds(start, lines.shape[1])] = lines[:channels].astype(BF16)

    synthesis(6, 0, write_out)
    first = pl.ds(0, 2 * STEP)
    store_0 = pltpu.make_async_copy(out_v.at[:, first], grad_hbm.at[0, :, first], out_sem.at[0])
    store_0.start()
    took(full, ne - 1, g_recv.at[3])
    sums = (full[...] * scale).reshape(2 * hid, LANES)
    g_in, g_out = sums[:hid].T, sums[hid:].T
    w_in_grad[...] = g_in[:channels]
    w_out_grad[...] = g_out[:channels]
    b_grad[...] = g_in[channels]
    for n in range(6):
        left(n)
    took(gt, ne - 1, g_send.at[0])
    took(red1, nx - 1, g_send.at[1])
    took(agx, nx - 1, g_send.at[2])
    took(full, ne - 1, g_send.at[3])

    synthesis(7, 1, write_out)
    second = pl.ds(2 * STEP, cols - 2 * STEP)
    store_1 = pltpu.make_async_copy(out_v.at[:, second], grad_hbm.at[0, :, second], out_sem.at[1])
    store_1.start()
    left(6)
    left(7)
    store_0.wait()
    store_1.wait()


def body(nx, nz, ne, state, cotangent, w_in, b_in, w_out, legendre, diffusion, quad, table):
    nb = nx * nz
    channels, cols = state.shape[1:]
    hid = w_in.shape[1]
    nlat = legendre.shape[1]
    modes = nb * LATS
    per_e = 2 * hid // ne
    per_x = per_e // nx
    steps = max(1, nz.bit_length() - 1)
    scale = 1.0 / math.sqrt(ne * nlat * NLON)
    any_spec = pl.BlockSpec(memory_space=pl.ANY)
    vmem = pl.BlockSpec(memory_space=pltpu.VMEM)
    smem = pl.BlockSpec(memory_space=pltpu.SMEM)
    dma = pltpu.SemaphoreType.DMA
    grad, g_in, g_out, g_b = pl.pallas_call(
        functools.partial(kernel, nx, nz, ne, scale),
        out_shape=(
            jax.ShapeDtypeStruct((1, channels, cols), BF16),
            jax.ShapeDtypeStruct((channels, hid), F32),
            jax.ShapeDtypeStruct((channels, hid), F32),
            jax.ShapeDtypeStruct((hid,), F32),
        ),
        in_specs=[any_spec] * 4 + [vmem] * 4 + [smem, vmem, smem, vmem],
        out_specs=(any_spec, vmem, vmem, vmem),
        scratch_shapes=[
            pltpu.VMEM((channels, cols), BF16),
            pltpu.VMEM((channels, cols), BF16),
            pltpu.VMEM((LATS, nlat, nlat), BF16),
            pltpu.VMEM((LATS, 2, modes, WINDOW), BF16),
            pltpu.VMEM((LATS, 2 * modes, WINDOW), BF16),
            pltpu.VMEM((LANES, cols), BF16),
            pltpu.VMEM((LANES, cols), BF16),
            pltpu.VMEM((LATS, nlat, nlat), BF16),
            pltpu.VMEM((LATS, nlat, nlat), BF16),
            pltpu.VMEM((max(1, nlat // LANES), nlat, min(LANES, nlat)), F32),
            pltpu.VMEM((LANES, hid), BF16),
            pltpu.VMEM((hid, LANES), BF16),
            pltpu.VMEM((hid, LANES), BF16),
            pltpu.VMEM((hid, LANES), F32),
            pltpu.VMEM((LATS, nlat, 2 * LANES), F32),
            pltpu.VMEM((2, nlat, LANES), F32),
            pltpu.VMEM((hid, cols), F32),
            pltpu.VMEM((LATS, 2 * modes, LANES), F32),
            pltpu.VMEM((nb * BLOCK, LANES), F32),
            pltpu.VMEM((nb * BLOCK, LANES), F32),
            pltpu.VMEM((LATS, nlat, 2 * LANES), F32),
            pltpu.VMEM((2, LANES, 2 * modes), BF16),
            pltpu.VMEM((LANES, LANES), F32),
            pltpu.VMEM((LANES, cols), BF16),
            pltpu.VMEM((hid, cols), BF16),
            pltpu.VMEM((hid, cols), BF16),
            pltpu.VMEM((LANES, cols), BF16),
            pltpu.VMEM((channels, cols), BF16),
            pltpu.VMEM((8, LANES), F32),
            pltpu.VMEM((LATS * nb, modes), BF16),
            pltpu.VMEM((8, nb, BLOCK, LANES), BF16),
            pltpu.VMEM((8, nb, BLOCK, LANES), BF16),
            pltpu.VMEM((ne, per_e, LANES), F32),
            pltpu.VMEM((ne, per_e, LANES), F32),
            pltpu.VMEM((nx, per_x, LANES), F32),
            pltpu.VMEM((nx, per_x, LANES), F32),
            pltpu.VMEM((steps, per_x, LANES), F32),
            pltpu.VMEM((steps, per_x, LANES), F32),
            pltpu.VMEM((nx, per_x, LANES), F32),
            pltpu.VMEM((ne, per_e, LANES), F32),
            dma((7,)),
            dma((2,)),
            dma((8,)),
            dma((8,)),
            dma((4,)),
            dma((4,)),
            dma((steps,)),
            dma((steps,)),
        ],
        compiler_params=pltpu.CompilerParams(
            collective_id=0, has_side_effects=True, vmem_limit_bytes=60 * 1024 * 1024
        ),
    )(
        state, cotangent, legendre, jnp.asarray(trig_table(modes)), w_in, w_out, b_in,
        diffusion.reshape(1, channels), quad, quad.reshape(1, nlat), table.T, table.T,
    )
    return grad, g_in, g_out, g_b


def solution(mesh):
    nb, ne = mesh.shape["band"], mesh.shape["ens"]
    nx = 4 if nb == 64 else 2
    placed = (
        P("ens", None, "band"),
        P("ens", None, "band"),
        P(),
        P(),
        P(),
        P("band", None, None),
        P(),
        P(),
        P(),
    )
    return jax.shard_map(
        functools.partial(body, nx, nb // nx, ne),
        mesh=mesh,
        in_specs=placed,
        out_specs=(P("ens", None, "band"), P(), P(), P()),
        check_vma=False,
    )
```

time: 159 us -> 148 us (0.931)
  Pallas kernels: 150 us -> 142 us
  local copies, waits for them, and re-layouts: 6.54 us -> 4.5 us
    pallas_call x1, Pallas kernels: 150 us -> 142 us  [body(): pl.pallas_call(functools.partial(kernel, nx, nz, ne, scale), out_shape=(j...]
    unnamed x8 -> x10, local copies, waits for them, and re-layouts: 5.3 us -> 4.5 us
where the time goes in v2:
time: 148 us
  Pallas kernels  142 us (96%)
  local copies, waits for them, and re-layouts  4.5 us (3%)
    pallas_call x1, Pallas kernels, body(): pl.pallas_call(functools.partial(kernel, nx, nz, ne, scale), out_shape=(j...  142 us
    unnamed x10, local copies, waits for them, and re-layouts  4.5 us

profile of v2, /device:TPU:1, one launch (start us, length us, event | category | flops | bytes accessed | tf_op | source)
XLA Modules:
  0.0 147.6 jit_solution(8641224356736450997)
XLA Ops:
  0.6 142.4 %shard_map.129 = (bf16[1,114,5760]{2,1,0:T(8,128)(2,1)}, f32[114,384]{1,0:T(8,128)}, f32[114,384]{1,0:T(8,128)}, f32[384]{0:T(512)}) custom-call(bf16[1,114,5760]{2,1,0:T(8,128)(2,1)} %state_hbm.1, bf16[1,114,5760]{2,1,0:T(8,128)(2,1)} %cot_hbm.1, bf16[4,256,256]{2,1,0:T(8,128)(2,1)} %leg_hbm.1, bf16[4,2,256,1536]{3,2,1,0:T(8,128)(2,1)} %constant.2.clone.trig_hbm, ...), custom_call_target="tpu_custom_call" | custom-call | tf_op jit(solution)/shard_map/pallas_call | solution.py:396
  143.1 0.0 copy-start.1
  143.1 0.0 copy-start
  143.1 0.0 copy-start.2
  143.1 2.6 %copy.18 = bf16[1,114,5760]{2,1,0:T(8,128)(2,1)} copy(bf16[1,114,5760]{2,1,0:T(8,128)(2,1)} %get-tuple-element.8) | data formatting | bytes 2626560
  145.7 0.0 copy-done.1
  145.7 0.7 copy.19
  146.3 0.0 copy-done
  146.4 0.7 copy.20
  147.0 0.0 copy-done.2
  147.0 0.6 copy.21
Async XLA Ops:
  143.1 2.6 %copy-start.1 = (f32[114,384]{1,0:T(8,128)S(1)}, f32[114,384]{1,0:T(8,128)}, u32[]{:S(2)}) copy-start(f32[114,384]{1,0:T(8,128)} %get-tuple-element.9) | copy-start | bytes 525316
  143.1 3.3 %copy-start = (f32[114,384]{1,0:T(8,128)S(1)}, f32[114,384]{1,0:T(8,128)}, u32[]{:S(2)}) copy-start(f32[114,384]{1,0:T(8,128)} %get-tuple-element.10) | copy-start | bytes 525316
  143.1 3.9 %copy-start.2 = (f32[384]{0:T(512)S(1)}, f32[384]{0:T(512)}, u32[]{:S(2)}) copy-start(f32[384]{0:T(512)} %get-tuple-element.11) | copy-start | bytes 4612

commit v3 on v2

--- a/solution.py
+++ b/solution.py
@@ -87,12 +87,11 @@
     lax.fori_loop(1, nb, greet_band, 0)
     lax.fori_loop(1, ne, greet_ens, 0)
 
-    def exchange(n, p):
+    def prepare(n, p):
         send[n] = stage[p][...].reshape(nb, BLOCK, LANES).astype(BF16)
         recv[n, pl.ds(me, 1)] = send[n, pl.ds(me, 1)]
-        if n == 0:
-            pl.semaphore_wait(barrier, nb - 1 + ne - 1)
-
+
+    def start(n, first, last):
         def one(i, _):
             peer = peer_of(nb - i)
             pltpu.make_async_remote_copy(
@@ -105,7 +104,7 @@
             ).start()
             return 0
 
-        lax.fori_loop(1, nb, one, 0)
+        lax.fori_loop(first, last, one, 0)
 
     def arrived(n, p):
         part = recv.at[n, pl.ds(0, nb - 1)]
@@ -151,7 +150,10 @@
                 s, r = k // 2, k % 2
                 at = (2 * sub + r) * LANES
                 stage[p][rows_of(sub, k), :] = picked[s * nb : (s + 1) * nb, at : at + LANES]
-        exchange(p, p)
+        prepare(p, p)
+        if p == 0:
+            pl.semaphore_wait(barrier, nb - 1 + ne - 1)
+        start(p, 1, nb)
 
     for a in range(LATS):
         for r in range(2):
@@ -201,7 +203,7 @@
 
     lax.fori_loop(0, 5, weigh, 0)
 
-    def legendre(n, weight):
+    def legendre(n, weight, between=None):
         def lines(p, s):
             parts = [
                 jnp.concatenate([stage[p][rows_of(sub, 2 * s + r), :] for sub in range(2)], axis=0)
@@ -212,6 +214,8 @@
         arrived(n, 0)
         for s in range(LATS):
             partial[s] = nn(leg_t[s, :, pl.ds(0, pair)], lines(0, s))
+        if between is not None:
+            between()
         arrived(n + 1, 1)
         spectrum = []
         for s in range(LATS):
@@ -226,7 +230,9 @@
                         part = part * quad_cols[1, pl.ds(p * pair, pair), :]
                     for sub in range(2):
                         stage[p][rows_of(sub, 2 * s + r), :] = part[sub * nb : (sub + 1) * nb]
-            exchange(n + 2 + p, p)
+            prepare(n + 2 + p, p)
+            if between is None:
+                start(n + 2 + p, 1, nb)
 
     def synthesis(n, p, write):
         arrived(n, p)
@@ -275,7 +281,8 @@
             coef = direct[a] + nt(wave[a], back_grid[:, window(a)])
             for k in range(8):
                 stage[p][rows_of(sub, k), :] = coef[k * nb : (k + 1) * nb]
-        exchange(4 + p, p)
+        prepare(4 + p, p)
+        start(4 + p, 1, nb if p == 0 else nb // 2)
 
     per_e = 2 * hid // ne
     per_x = per_e // nx
@@ -312,13 +319,28 @@
 
         lax.fori_loop(1, nx, one, 0)
 
-    def to_z(step):
-        distance = 1 << step
-        partner = my_z + distance * (1 - 2 * lax.rem(my_z // distance, 2))
-        return pltpu.make_async_remote_copy(
-            src_ref=zsend.at[step], dst_ref=zrecv.at[step], send_sem=z_send.at[step],
-            recv_sem=z_recv.at[step], device_id=(my_x * nz + partner, ens), device_id_type=MESH,
-        )
+    z_sizes = (4, nz // 4)
+
+    def to_z(step, value):
+        stride = 4**step
+        digit = lax.rem(my_z // stride, z_sizes[step])
+        zrecv[step, pl.ds(digit, 1)] = value[None]
+        zsend[step] = value
+
+        def one(i, _):
+            other = my_z + (lax.rem(digit + i, z_sizes[step]) - digit) * stride
+            pltpu.make_async_remote_copy(
+                src_ref=zsend.at[step], dst_ref=zrecv.at[step, digit], send_sem=z_send.at[step],
+                recv_sem=z_recv.at[step], device_id=(my_x * nz + other, ens), device_id_type=MESH,
+            ).start()
+            return 0
+
+        lax.fori_loop(1, z_sizes[step], one, 0)
+
+    def from_z(step):
+        if z_sizes[step] > 1:
+            took(zrecv.at[step], z_sizes[step] - 1, z_recv.at[step])
+        return jnp.sum(zrecv[step, pl.ds(0, z_sizes[step])], axis=0)
 
     def took(ref, count, sem):
         part = ref.at[pl.ds(0, count)]
@@ -326,28 +348,28 @@
 
     rs1[pl.ds(ens, 1)] = gt[pl.ds(ens, 1)]
     to_ens(lambda other: gt.at[other], rs1.at[ens], 0)
-    took(rs1, ne - 1, g_recv.at[0])
-    red1[...] = jnp.sum(rs1[...], axis=0).reshape(nx, per_x, LANES)
-    rs2[pl.ds(my_x, 1)] = red1[pl.ds(my_x, 1)]
-    to_x(lambda other: red1.at[other], rs2.at[my_x], 1)
+    start(5, nb // 2, nb)
+
+    def scatter_x():
+        took(rs1, ne - 1, g_recv.at[0])
+        red1[...] = jnp.sum(rs1[...], axis=0).reshape(nx, per_x, LANES)
+        rs2[pl.ds(my_x, 1)] = red1[pl.ds(my_x, 1)]
+        to_x(lambda other: red1.at[other], rs2.at[my_x], 1)
+
+    legendre(4, True, scatter_x)
+    start(6, 1, nb // 4)
     took(rs2, nx - 1, g_recv.at[1])
-    zsend[0] = jnp.sum(rs2[...], axis=0)
-    to_z(0).start()
-
-    legendre(4, True)
-
-    steps = nz.bit_length() - 1
-    for step in range(steps):
-        to_z(step).wait()
-        total = zsend[step] + zrecv[step]
-        if step + 1 < steps:
-            zsend[step + 1] = total
-            to_z(step + 1).start()
-    agx[pl.ds(my_x, 1)] = total[None]
+    to_z(0, jnp.sum(rs2[...], axis=0))
+    start(6, nb // 4, nb // 2)
+    to_z(1, from_z(0))
+    start(6, nb // 2, nb)
+    agx[pl.ds(my_x, 1)] = from_z(1)[None]
     to_x(lambda other: agx.at[my_x], agx.at[my_x], 2)
+    start(7, 1, nb // 2)
     took(agx, nx - 1, g_recv.at[2])
     full[pl.ds(ens, 1)] = agx[...].reshape(1, per_e, LANES)
     to_ens(lambda other: full.at[ens], full.at[ens], 3)
+    start(7, nb // 2, nb)
 
     def write_out(start, lines):
         out_v[:, pl.ds(start, lines.shape[1])] = lines[:channels].astype(BF16)
@@ -368,6 +390,9 @@
     took(red1, nx - 1, g_send.at[1])
     took(agx, nx - 1, g_send.at[2])
     took(full, ne - 1, g_send.at[3])
+    for step in range(2):
+        if z_sizes[step] > 1:
+            took(zrecv.at[step], z_sizes[step] - 1, z_send.at[step])
 
     synthesis(7, 1, write_out)
     second = pl.ds(2 * STEP, cols - 2 * STEP)
@@ -387,7 +412,6 @@
     modes = nb * LATS
     per_e = 2 * hid // ne
     per_x = per_e // nx
-    steps = max(1, nz.bit_length() - 1)
     scale = 1.0 / math.sqrt(ne * nlat * NLON)
     any_spec = pl.BlockSpec(memory_space=pl.ANY)
     vmem = pl.BlockSpec(memory_space=pltpu.VMEM)
@@ -440,8 +464,8 @@
             pltpu.VMEM((ne, per_e, LANES), F32),
             pltpu.VMEM((nx, per_x, LANES), F32),
             pltpu.VMEM((nx, per_x, LANES), F32),
-            pltpu.VMEM((steps, per_x, LANES), F32),
-            pltpu.VMEM((steps, per_x, LANES), F32),
+            pltpu.VMEM((2, per_x, LANES), F32),
+            pltpu.VMEM((2, 4, per_x, LANES), F32),
             pltpu.VMEM((nx, per_x, LANES), F32),
             pltpu.VMEM((ne, per_e, LANES), F32),
             dma((7,)),
@@ -450,8 +474,8 @@
             dma((8,)),
             dma((4,)),
             dma((4,)),
-            dma((steps,)),
-            dma((steps,)),
+            dma((2,)),
+            dma((2,)),
         ],
         compiler_params=pltpu.CompilerParams(
             collective_id=0, has_side_effects=True, vmem_limit_bytes=60 * 1024 * 1024

time: 148 us -> 132 us (0.89)
  the two profiles are of different devices: /device:TPU:1 before, /device:TPU:8 now
where the time goes in v3:
time: 132 us
  Pallas kernels  127 us (96%)
  local copies, waits for them, and re-layouts  4.5 us (3%)
    pallas_call x1, Pallas kernels, body(): pl.pallas_call(functools.partial(kernel, nx, nz, ne, scale), out_shape=(j...  127 us
    unnamed x10, local copies, waits for them, and re-layouts  4.5 us

profile of v3, /device:TPU:8, one launch (start us, length us, event | category | flops | bytes accessed | tf_op | source)
XLA Modules:
  0.0 132.3 jit_solution(11785524619963246512)
XLA Ops:
  0.6 127.1 %shard_map.129 = (bf16[1,114,5760]{2,1,0:T(8,128)(2,1)}, f32[114,384]{1,0:T(8,128)}, f32[114,384]{1,0:T(8,128)}, f32[384]{0:T(512)}) custom-call(bf16[1,114,5760]{2,1,0:T(8,128)(2,1)} %state_hbm.1, bf16[1,114,5760]{2,1,0:T(8,128)(2,1)} %cot_hbm.1, bf16[4,256,256]{2,1,0:T(8,128)(2,1)} %leg_hbm.1, bf16[4,2,256,1536]{3,2,1,0:T(8,128)(2,1)} %constant.2.clone.trig_hbm, ...), custom_call_target="tpu_custom_call" | custom-call | tf_op jit(solution)/shard_map/pallas_call | solution.py:420
  127.8 0.0 copy-start.1
  127.8 0.0 copy-start
  127.8 0.0 copy-start.2
  127.8 2.6 %copy.18 = bf16[1,114,5760]{2,1,0:T(8,128)(2,1)} copy(bf16[1,114,5760]{2,1,0:T(8,128)(2,1)} %get-tuple-element.8) | data formatting | bytes 2626560
  130.4 0.0 copy-done.1
  130.4 0.7 copy.19
  131.1 0.0 copy-done
  131.1 0.7 copy.20
  131.7 0.0 copy-done.2
  131.7 0.6 copy.21
Async XLA Ops:
  127.8 2.6 %copy-start.1 = (f32[114,384]{1,0:T(8,128)S(1)}, f32[114,384]{1,0:T(8,128)}, u32[]{:S(2)}) copy-start(f32[114,384]{1,0:T(8,128)} %get-tuple-element.9) | copy-start | bytes 525316
  127.8 3.3 %copy-start = (f32[114,384]{1,0:T(8,128)S(1)}, f32[114,384]{1,0:T(8,128)}, u32[]{:S(2)}) copy-start(f32[114,384]{1,0:T(8,128)} %get-tuple-element.10) | copy-start | bytes 525316
  127.8 3.9 %copy-start.2 = (f32[384]{0:T(512)S(1)}, f32[384]{0:T(512)}, u32[]{:S(2)}) copy-start(f32[384]{0:T(512)} %get-tuple-element.11) | copy-start | bytes 4612

commit v4 on v3

--- a/solution.py
+++ b/solution.py
@@ -65,7 +65,7 @@
     load_trig = [pltpu.make_async_copy(trig_hbm.at[a], trig.at[a], in_sem.at[1 + a]) for a in range(LATS)]
     load_cot = pltpu.make_async_copy(cot_hbm.at[0], cot_raw, in_sem.at[5])
     load_leg = pltpu.make_async_copy(leg_hbm, leg_raw, in_sem.at[6])
-    for load in (load_state, *load_trig, load_cot, load_leg):
+    for load in (load_state, *load_trig[:2]):
         load.start()
 
     def peer_of(i):
@@ -141,6 +141,9 @@
         for sub in range(2):
             a = 2 * p + sub
             load_trig[a].wait()
+            if a == 1:
+                for load in (*load_trig[2:], load_leg, load_cot):
+                    load.start()
             coef = nt(trig[a].reshape(2 * modes, WINDOW), state_pad[:, window(a)])
             coef = (coef * quad[me * LATS + a]).astype(BF16)
             pieces += [coef[:modes], coef[modes:]]
@@ -203,7 +206,7 @@
 
     lax.fori_loop(0, 5, weigh, 0)
 
-    def legendre(n, weight, between=None):
+    def legendre(n, weight, between=None, first=nb):
         def lines(p, s):
             parts = [
                 jnp.concatenate([stage[p][rows_of(sub, 2 * s + r), :] for sub in range(2)], axis=0)
@@ -231,8 +234,8 @@
                     for sub in range(2):
                         stage[p][rows_of(sub, 2 * s + r), :] = part[sub * nb : (sub + 1) * nb]
             prepare(n + 2 + p, p)
-            if between is None:
-                start(n + 2 + p, 1, nb)
+            if p == 0 or between is None:
+                start(n + 2 + p, 1, first)
 
     def synthesis(n, p, write):
         arrived(n, p)
@@ -268,6 +271,20 @@
         back_grid[:, at] = nn(w_in_pad[...], grad).astype(BF16)
         return 0
 
+    per_e = 2 * hid // ne
+    per_x = per_e // nx
+    gt[...] = jnp.zeros_like(gt)
+
+    def gradients(begin, width):
+        def one(i, _):
+            at = pl.ds(pl.multiple_of(begin + i * width, LANES), width)
+            g_in = nt(pre_grad[:, at], y[:, at])
+            g_out = nt(hidden[:, at], cot_pad[:, at])
+            gt[...] += jnp.concatenate([g_in, g_out], axis=0).reshape(gt.shape)
+            return 0
+
+        lax.fori_loop(0, 3, one, 0)
+
     y[:, pl.ds(2 * STEP + LANES, LANES)] = jnp.zeros((LANES, LANES), BF16)
     tiles = cols // LANES
     per_pair, per_chunk = (tiles + 1) // 2, CHUNK // LANES
@@ -282,20 +299,11 @@
             for k in range(8):
                 stage[p][rows_of(sub, k), :] = coef[k * nb : (k + 1) * nb]
         prepare(4 + p, p)
-        start(4 + p, 1, nb if p == 0 else nb // 2)
-
-    per_e = 2 * hid // ne
-    per_x = per_e // nx
-    gt[...] = jnp.zeros_like(gt)
-
-    def gradients(i, _):
-        at = pl.ds(pl.multiple_of(i * wide, LANES), wide)
-        g_in = nt(pre_grad[:, at], y[:, at])
-        g_out = nt(hidden[:, at], cot_pad[:, at])
-        gt[...] += jnp.concatenate([g_in, g_out], axis=0).reshape(gt.shape)
-        return 0
-
-    lax.fori_loop(0, 5, gradients, 0)
+        if p == 0:
+            start(4, 1, nb)
+            gradients(0, (tiles - trips * per_chunk) * LANES // 3)
+        else:
+            gradients(begin * LANES, trips * CHUNK // 3)
 
     def to_ens(src, dst, n):
         def one(i, _):
@@ -348,23 +356,23 @@
 
     rs1[pl.ds(ens, 1)] = gt[pl.ds(ens, 1)]
     to_ens(lambda other: gt.at[other], rs1.at[ens], 0)
-    start(5, nb // 2, nb)
-
-    def scatter_x():
-        took(rs1, ne - 1, g_recv.at[0])
-        red1[...] = jnp.sum(rs1[...], axis=0).reshape(nx, per_x, LANES)
-        rs2[pl.ds(my_x, 1)] = red1[pl.ds(my_x, 1)]
-        to_x(lambda other: red1.at[other], rs2.at[my_x], 1)
-
-    legendre(4, True, scatter_x)
-    start(6, 1, nb // 4)
-    took(rs2, nx - 1, g_recv.at[1])
-    to_z(0, jnp.sum(rs2[...], axis=0))
-    start(6, nb // 4, nb // 2)
+    start(5, 1, 5 * nb // 8)
+    took(rs1, ne - 1, g_recv.at[0])
+    red1[...] = jnp.sum(rs1[...], axis=0).reshape(nx, per_x, LANES)
+    rs2[pl.ds(my_x, 1)] = red1[pl.ds(my_x, 1)]
+    to_x(lambda other: red1.at[other], rs2.at[my_x], 1)
+    start(5, 5 * nb // 8, nb)
+
+    def first_z():
+        took(rs2, nx - 1, g_recv.at[1])
+        to_z(0, jnp.sum(rs2[...], axis=0))
+
+    legendre(4, True, first_z, 3 * nb // 8)
     to_z(1, from_z(0))
-    start(6, nb // 2, nb)
+    start(6, 3 * nb // 8, 7 * nb // 8)
     agx[pl.ds(my_x, 1)] = from_z(1)[None]
     to_x(lambda other: agx.at[my_x], agx.at[my_x], 2)
+    start(6, 7 * nb // 8, nb)
     start(7, 1, nb // 2)
     took(agx, nx - 1, g_recv.at[2])
     full[pl.ds(ens, 1)] = agx[...].reshape(1, per_e, LANES)

time: 132 us -> 131 us (level)
  the two profiles are of different devices: /device:TPU:8 before, /device:TPU:1 now
where the time goes in v4:
time: 131 us; the launch traced here: 130 us
  Pallas kernels  125 us (95%)
  local copies, waits for them, and re-layouts  4.5 us (3%)
    pallas_call x1, Pallas kernels, body(): pl.pallas_call(functools.partial(kernel, nx, nz, ne, scale), out_shape=(j...  125 us
    unnamed x10, local copies, waits for them, and re-layouts  4.5 us

profile of v4, /device:TPU:1, one launch (start us, length us, event | category | flops | bytes accessed | tf_op | source)
XLA Modules:
  0.0 130.5 jit_solution(6115614152957011681)
XLA Ops:
  0.6 125.3 %shard_map.129 = (bf16[1,114,5760]{2,1,0:T(8,128)(2,1)}, f32[114,384]{1,0:T(8,128)}, f32[114,384]{1,0:T(8,128)}, f32[384]{0:T(512)}) custom-call(bf16[1,114,5760]{2,1,0:T(8,128)(2,1)} %state_hbm.1, bf16[1,114,5760]{2,1,0:T(8,128)(2,1)} %cot_hbm.1, bf16[4,256,256]{2,1,0:T(8,128)(2,1)} %leg_hbm.1, bf16[4,2,256,1536]{3,2,1,0:T(8,128)(2,1)} %constant.2.clone.trig_hbm, ...), custom_call_target="tpu_custom_call" | custom-call | tf_op jit(solution)/shard_map/pallas_call | solution.py:428
  126.0 0.0 copy-start.1
  126.0 0.0 copy-start
  126.0 0.0 copy-start.2
  126.0 2.6 %copy.18 = bf16[1,114,5760]{2,1,0:T(8,128)(2,1)} copy(bf16[1,114,5760]{2,1,0:T(8,128)(2,1)} %get-tuple-element.8) | data formatting | bytes 2626560
  128.6 0.0 copy-done.1
  128.6 0.7 copy.19
  129.2 0.0 copy-done
  129.2 0.7 copy.20
  129.9 0.0 copy-done.2
  129.9 0.6 copy.21
Async XLA Ops:
  126.0 2.6 %copy-start.1 = (f32[114,384]{1,0:T(8,128)S(1)}, f32[114,384]{1,0:T(8,128)}, u32[]{:S(2)}) copy-start(f32[114,384]{1,0:T(8,128)} %get-tuple-element.9) | copy-start | bytes 525316
  126.0 3.3 %copy-start = (f32[114,384]{1,0:T(8,128)S(1)}, f32[114,384]{1,0:T(8,128)}, u32[]{:S(2)}) copy-start(f32[114,384]{1,0:T(8,128)} %get-tuple-element.10) | copy-start | bytes 525316
  126.0 3.9 %copy-start.2 = (f32[384]{0:T(512)S(1)}, f32[384]{0:T(512)}, u32[]{:S(2)}) copy-start(f32[384]{0:T(512)} %get-tuple-element.11) | copy-start | bytes 4612

commit v5 on v4

--- a/solution.py
+++ b/solution.py
@@ -40,9 +40,9 @@
 
 
 def kernel(
-    nx, nz, ne, scale,
+    nx, nz, ne,
     state_hbm, cot_hbm, leg_hbm, trig_hbm, w_in, w_out, bias, diffusion, quad, quad_row, table, table_v,
-    grad_hbm, w_in_grad, w_out_grad, b_grad,
+    head_hbm, lines_hbm, tail_hbm, wave_hbm, sums_hbm,
     state_raw, cot_raw, leg_raw, trig, wave, state_pad, cot_pad, leg, leg_t, leg_f, w_in_pad, w_in_t, w_out_t, b_cols,
     keep, quad_cols, hidden_grad, direct, stage_0, stage_1, partial, back_t, tail, y, hidden, pre_grad, back_grid,
     out_v, small, picks, send, recv, gt, rs1, red1, rs2, zsend, zrecv, agx, full,
@@ -237,11 +237,14 @@
             if p == 0 or between is None:
                 start(n + 2 + p, 1, first)
 
-    def synthesis(n, p, write):
+    def gather(n, p):
         arrived(n, p)
         for sub in range(2):
             rows = jnp.concatenate([stage[p][rows_of(sub, k), :] for k in range(8)], axis=0)
             back_t[sub] = rows.T.astype(BF16)
+
+    def synthesis(n, p, write):
+        gather(n, p)
         held = tail[...] if p else None
         for sub in range(2):
             a = 2 * p + sub
@@ -382,16 +385,16 @@
     def write_out(start, lines):
         out_v[:, pl.ds(start, lines.shape[1])] = lines[:channels].astype(BF16)
 
+    keep_wave = pltpu.make_async_copy(wave.at[pl.ds(2, 2)], wave_hbm, out_sem.at[0])
+    keep_wave.start()
     synthesis(6, 0, write_out)
-    first = pl.ds(0, 2 * STEP)
-    store_0 = pltpu.make_async_copy(out_v.at[:, first], grad_hbm.at[0, :, first], out_sem.at[0])
-    store_0.start()
+    head = pltpu.make_async_copy(out_v.at[:, pl.ds(0, 2 * STEP)], head_hbm, out_sem.at[1])
+    head.start()
+    keep_tail = pltpu.make_async_copy(tail, tail_hbm, out_sem.at[2])
+    keep_tail.start()
     took(full, ne - 1, g_recv.at[3])
-    sums = (full[...] * scale).reshape(2 * hid, LANES)
-    g_in, g_out = sums[:hid].T, sums[hid:].T
-    w_in_grad[...] = g_in[:channels]
-    w_out_grad[...] = g_out[:channels]
-    b_grad[...] = g_in[channels]
+    keep_sums = pltpu.make_async_copy(full, sums_hbm, out_sem.at[3])
+    keep_sums.start()
     for n in range(6):
         left(n)
     took(gt, ne - 1, g_send.at[0])
@@ -401,13 +404,60 @@
     for step in range(2):
         if z_sizes[step] > 1:
             took(zrecv.at[step], z_sizes[step] - 1, z_send.at[step])
-
-    synthesis(7, 1, write_out)
-    second = pl.ds(2 * STEP, cols - 2 * STEP)
-    store_1 = pltpu.make_async_copy(out_v.at[:, second], grad_hbm.at[0, :, second], out_sem.at[1])
-    store_1.start()
     left(6)
     left(7)
+    keep_wave.wait()
+    head.wait()
+    keep_tail.wait()
+    keep_sums.wait()
+    gather(7, 1)
+    keep_lines = pltpu.make_async_copy(back_t, lines_hbm, out_sem.at[4])
+    keep_lines.start()
+    keep_lines.wait()
+
+
+def last_kernel(
+    scale, head_hbm, lines_hbm, tail_hbm, wave_hbm, sums_hbm, grad_hbm, w_in_grad, w_out_grad, b_grad,
+    lines_v, tail, wave, sums, out_v, sem,
+):
+    channels = out_v.shape[0]
+    hid = w_in_grad.shape[1]
+    front, rear = pl.ds(0, 2 * STEP), pl.ds(2 * STEP, out_v.shape[1] - 2 * STEP)
+    head = pltpu.make_async_copy(head_hbm, out_v.at[:, front], sem.at[0])
+    store_0 = pltpu.make_async_copy(out_v.at[:, front], grad_hbm.at[0, :, front], sem.at[7])
+    store_1 = pltpu.make_async_copy(out_v.at[:, rear], grad_hbm.at[0, :, rear], sem.at[6])
+    loads = [
+        pltpu.make_async_copy(lines_hbm, lines_v, sem.at[1]),
+        pltpu.make_async_copy(wave_hbm.at[0], wave.at[0], sem.at[2]),
+        pltpu.make_async_copy(tail_hbm, tail, sem.at[3]),
+        pltpu.make_async_copy(wave_hbm.at[1], wave.at[1], sem.at[4]),
+        pltpu.make_async_copy(sums_hbm, sums, sem.at[5]),
+    ]
+    for load in loads:
+        load.start()
+    head.start()
+    loads[0].wait()
+    loads[1].wait()
+    loads[2].wait()
+    held = tail[...]
+    for sub in range(2):
+        if sub == 1:
+            head.wait()
+            store_0.start()
+            loads[3].wait()
+        lines = nn(lines_v[sub], wave[sub])
+        first = (lines[:, :LANES] + held)[:channels].astype(BF16)
+        out_v[:, pl.ds((2 + sub) * STEP, LANES)] = first
+        out_v[:, pl.ds((2 + sub) * STEP + LANES, STEP - LANES)] = lines[:channels, LANES:STEP].astype(BF16)
+        held = lines[:, STEP:]
+    out_v[:, pl.ds(4 * STEP, LANES)] = held[:channels].astype(BF16)
+    store_1.start()
+    loads[4].wait()
+    scaled = (sums[...] * scale).reshape(2 * hid, LANES)
+    g_in, g_out = scaled[:hid].T, scaled[hid:].T
+    w_in_grad[...] = g_in[:channels]
+    w_out_grad[...] = g_out[:channels]
+    b_grad[...] = g_in[channels]
     store_0.wait()
     store_1.wait()
 
@@ -425,16 +475,17 @@
     vmem = pl.BlockSpec(memory_space=pltpu.VMEM)
     smem = pl.BlockSpec(memory_space=pltpu.SMEM)
     dma = pltpu.SemaphoreType.DMA
-    grad, g_in, g_out, g_b = pl.pallas_call(
-        functools.partial(kernel, nx, nz, ne, scale),
+    parts = pl.pallas_call(
+        functools.partial(kernel, nx, nz, ne),
         out_shape=(
-            jax.ShapeDtypeStruct((1, channels, cols), BF16),
-            jax.ShapeDtypeStruct((channels, hid), F32),
-            jax.ShapeDtypeStruct((channels, hid), F32),
-            jax.ShapeDtypeStruct((hid,), F32),
+            jax.ShapeDtypeStruct((channels, 2 * STEP), BF16),
+            jax.ShapeDtypeStruct((2, LANES, 2 * modes), BF16),
+            jax.ShapeDtypeStruct((LANES, LANES), F32),
+            jax.ShapeDtypeStruct((2, 2 * modes, WINDOW), BF16),
+            jax.ShapeDtypeStruct((ne, per_e, LANES), F32),
         ),
         in_specs=[any_spec] * 4 + [vmem] * 4 + [smem, vmem, smem, vmem],
-        out_specs=(any_spec, vmem, vmem, vmem),
+        out_specs=(any_spec,) * 5,
         scratch_shapes=[
             pltpu.VMEM((channels, cols), BF16),
             pltpu.VMEM((channels, cols), BF16),
@@ -477,7 +528,7 @@
             pltpu.VMEM((nx, per_x, LANES), F32),
             pltpu.VMEM((ne, per_e, LANES), F32),
             dma((7,)),
-            dma((2,)),
+            dma((5,)),
             dma((8,)),
             dma((8,)),
             dma((4,)),
@@ -492,7 +543,26 @@
         state, cotangent, legendre, jnp.asarray(trig_table(modes)), w_in, w_out, b_in,
         diffusion.reshape(1, channels), quad, quad.reshape(1, nlat), table.T, table.T,
     )
-    return grad, g_in, g_out, g_b
+    return pl.pallas_call(
+        functools.partial(last_kernel, scale),
+        out_shape=(
+            jax.ShapeDtypeStruct((1, channels, cols), BF16),
+            jax.ShapeDtypeStruct((channels, hid), F32),
+            jax.ShapeDtypeStruct((channels, hid), F32),
+            jax.ShapeDtypeStruct((hid,), F32),
+        ),
+        in_specs=[any_spec] * 5,
+        out_specs=(any_spec, vmem, vmem, vmem),
+        scratch_shapes=[
+            pltpu.VMEM((2, LANES, 2 * modes), BF16),
+            pltpu.VMEM((LANES, LANES), F32),
+            pltpu.VMEM((2, 2 * modes, WINDOW), BF16),
+            pltpu.VMEM((ne, per_e, LANES), F32),
+            pltpu.VMEM((channels, cols), BF16),
+            dma((8,)),
+        ],
+        compiler_params=pltpu.CompilerParams(vmem_limit_bytes=60 * 1024 * 1024),
+    )(*parts)
 
 
 def solution(mesh):

time: 131 us -> 129 us (0.985)
  local copies, waits for them, and re-layouts: 4.5 us -> 0 us
  Pallas kernels: 125 us -> 128 us
    unnamed x10 -> x0, local copies, waits for them, and re-layouts: 4.5 us -> none
    pallas_call x1 -> x2, Pallas kernels: 125 us -> 128 us  [the longest x1 124 us: body(): pl.pallas_call(functools.partial(kernel, nx, nz, ne), out_shape=(jax.Shap...]
where the time goes in v5:
time: 129 us
  Pallas kernels  128 us (99%)
    pallas_call x1, Pallas kernels, body(): pl.pallas_call(functools.partial(kernel, nx, nz, ne), out_shape=(jax.Shap...  124 us
    pallas_call x1, Pallas kernels, body(): pl.pallas_call(functools.partial(last_kernel, scale), out_shape=(jax.Shap...  4.3 us

profile of v5, /device:TPU:1, one launch (start us, length us, event | category | flops | bytes accessed | tf_op | source)
XLA Modules:
  0.0 129.1 jit_solution(6170067307511761320)
XLA Ops:
  0.6 124.0 %shard_map.129 = (bf16[114,2816]{1,0:T(8,128)(2,1)}, bf16[2,128,512]{2,1,0:T(8,128)(2,1)}, f32[128,128]{1,0:T(8,128)}, bf16[2,512,1536]{2,1,0:T(8,128)(2,1)}, f32[8,96,128]{2,1,0:T(8,128)}) custom-call(bf16[1,114,5760]{2,1,0:T(8,128)(2,1)} %state_hbm.1, bf16[1,114,5760]{2,1,0:T(8,128)(2,1)} %cot_hbm.1, bf16[4,256,256]{2,1,0:T(8,128)(2,1)} %leg_hbm.1, ...), custom_call_target="tpu_custom_call" | custom-call | tf_op jit(solution)/shard_map/pallas_call | solution.py:478
  124.6 4.3 %shard_map.130 = (bf16[1,114,5760]{2,1,0:T(8,128)(2,1)}, f32[114,384]{1,0:T(8,128)}, f32[114,384]{1,0:T(8,128)}, f32[384]{0:T(512)}) custom-call(bf16[114,2816]{1,0:T(8,128)(2,1)} %get-tuple-element.9.head_hbm, bf16[2,128,512]{2,1,0:T(8,128)(2,1)} %get-tuple-element.10.lines_hbm, f32[128,128]{1,0:T(8,128)} %get-tuple-element.11.tail_hbm, ...), custom_call_target="tpu_custom_call" | custom-call | tf_op jit(solution)/shard_map/pallas_call | solution.py:546
